TPU v7x, 32 devices: a whole 2x2x4 slice. The times are simulated.
32 devices in a mesh: dp: 2 (over x), expert: 16 (over z, y, core).
Axes of the slice: x: 2, y: 2, z: 4, core: 2. Of those that a mesh axis runs over, the one named last changes fastest.
Arguments:
- tokens: bfloat16 [2048, 2048], P('expert'), may hold values from -6 to 6
- expert_ids: int32 [2048, 6], P('expert'), may hold values from 0 to 15, all different within a row; in each aligned block of 128 rows (0 to 127, 128 to 255, ...) at most 60 rows name the same one
- gates: float32 [2048, 6], P('expert'), may hold values from 0.05 to 0.5
- w_gate: bfloat16 [16, 2048, 1408], P('expert', None, 'dp'), may hold values from -0.125 to 0.125
- w_up: bfloat16 [16, 2048, 1408], P('expert', None, 'dp'), may hold values from -0.125 to 0.125
- w_down: bfloat16 [16, 1408, 2048], P('expert', 'dp'), may hold values from -0.15625 to 0.15625
- s_gate: bfloat16 [2048, 2816], P(None, 'dp'), may hold values from -0.125 to 0.125
- s_up: bfloat16 [2048, 2816], P(None, 'dp'), may hold values from -0.125 to 0.125
- s_down: bfloat16 [2816, 2048], P('dp'), may hold values from -0.109375 to 0.109375
- cotangent: bfloat16 [2048, 2048], P('expert'), may hold values from -6 to 6
Outputs:
- moe_out: bfloat16 [2048, 2048], P('expert')
- token_grads: bfloat16 [2048, 2048], P('expert')
- gate_grads: float32 [2048, 6], P('expert')
- grad_w_gate: bfloat16 [16, 2048, 1408], P('expert', None, 'dp')
- grad_w_up: bfloat16 [16, 2048, 1408], P('expert', None, 'dp')
- grad_w_down: bfloat16 [16, 1408, 2048], P('expert', 'dp')
- grad_s_gate: bfloat16 [2048, 2816], P('expert', 'dp')
- grad_s_up: bfloat16 [2048, 2816], P('expert', 'dp')
- grad_s_down: bfloat16 [2816, 2048], P('dp', 'expert')
Inputs may be any that keep to these rules, and one draw needn't show every extreme that they name: `expert_ids`: each row names 6 different experts. In each aligned block of 128 rows (the rows of one index of the expert axis) no expert is named by more than 60 rows, and in some block one expert is named by exactly 60 rows.
All inputs are finite; a program needn't handle non-finite values.
Results may differ from a plain program's by a relative error of at most 0.02.
Values may be sent and summed in bfloat16 or wider, within the bound.
No kernel may reach another device: no remote copies, remote signals or barrier semaphores. Data moves between devices by JAX's collectives and lax.ppermute only.
A program may use at most 192 MiB of HBM per device.

v0:
```python
import functools

import jax
import jax.numpy as jnp
import numpy as np
from jax import lax
from jax.experimental import pallas as pl
from jax.experimental.pallas import tpu as pltpu
from jax.sharding import PartitionSpec as P

F32 = jnp.float32
BF16 = jnp.bfloat16
GROUP = 4
VMEM_LIMIT = 56 * 1024 * 1024


def mm(left, right, left_dim, right_dim):
    return lax.dot_general(
        left, right, (((left_dim,), (right_dim,)), ((), ())), preferred_element_type=F32
    )


def split_of(experts, dp):
    bits = experts.bit_length() - 1
    middle = (bits - 1) // 2
    return (2, 1 << middle, 1 << (bits - 1 - middle), dp)


def partner(array, sizes, dim, k):
    if dim == 3:
        axis, mask = "dp", k
    else:
        axis, mask = "expert", k * (1, 2, 2 * sizes[1])[dim]
    return lax.ppermute(array, axis, [(i, i ^ mask) for i in range(lax.axis_size(axis))])


def after(arrays, *earlier):
    return lax.optimization_barrier((arrays, earlier))[0]


def spread(out, sizes, dim, *earlier):
    came = [partner(out, sizes, dim, k) for k in range(1, sizes[dim])]
    return jnp.concatenate([out] + after(came, *earlier), axis=dim)


def total(terms):
    out = terms[0].astype(F32)
    for term in terms[1:]:
        out = out + term.astype(F32)
    return out.astype(BF16)


def fold(terms, sizes, dim, *earlier):
    cut = lambda k: [lax.slice_in_dim(t, k, k + 1, axis=dim) for t in terms]
    came = [partner(total(cut(k)), sizes, dim, k) for k in range(1, sizes[dim])]
    return cut(0) + after(came, *earlier)


def both_halves(rows, sizes):
    out = [rows] + [partner(rows, sizes, 3, k) for k in range(1, sizes[3])]
    out = jnp.stack(out)
    order = jnp.arange(sizes[3]) ^ lax.axis_index("dp")
    return out[order].reshape(-1, rows.shape[1])


def pick_of(place_ref, gate_ref, rows):
    place = place_ref[0]
    hit = lax.broadcasted_iota(jnp.int32, (rows, place.shape[1]), 0) == place
    gate = jnp.sum(jnp.where(hit, gate_ref[0], 0.0), axis=1, keepdims=True)
    return hit, hit.astype(BF16), gate


def take_rows(pick, a_ref, b_ref, rows_ref):
    rows, tokens = pick.shape
    parts = GROUP // 2
    half = a_ref.shape[1]
    for i in range(parts):
        r = slice(i * rows // parts, (i + 1) * rows // parts)
        t = slice(i * tokens // parts, (i + 1) * tokens // parts)
        rows_ref[r, :half] = mm(pick[r, t], a_ref[t, :], 1, 0).astype(BF16)
        rows_ref[r, half:] = mm(pick[r, t], b_ref[t, :], 1, 0).astype(BF16)


def put_rows(pick, rows, units, weight_ref, a_ref, b_ref):
    half = a_ref.shape[1]
    left = jnp.concatenate([pick.T, units], axis=1)
    for ref, cut in ((a_ref, slice(0, half)), (b_ref, slice(half, 2 * half))):
        right = jnp.concatenate([rows[:, cut], weight_ref[:, cut]], axis=0)
        ref[...] = mm(left, right, 1, 0).astype(BF16)


def fetch(sources, targets, sems):
    copies = [
        pltpu.make_async_copy(src.at[0], dst, sems.at[i])
        for i, (src, dst) in enumerate(zip(sources, targets))
    ]

    @pl.when(pl.program_id(0) == 0)
    def _():
        for copy in copies:
            copy.start()

    def ready(*which):
        @pl.when(pl.program_id(0) == 0)
        def _():
            for i in which:
                copies[i].wait()

    return ready


def forward_kernel(
    place_ref, gate_ref, xa_ref, xb_ref, wg_hbm, wu_hbm, wd_hbm, sgu_ref, sd_ref,
    oa_ref, ob_ref, xr_ref, gp_ref, up_ref, hid_ref, spre_ref, shid_ref,
    wg_ref, wu_ref, wd_ref, sems,
):
    ready = fetch((wg_hbm, wu_hbm, wd_hbm), (wg_ref, wu_ref, wd_ref), sems)
    hit, pick, gate = pick_of(place_ref, gate_ref, xr_ref.shape[0])
    half = xa_ref.shape[1]
    unit = sd_ref.shape[0]
    take_rows(pick, xa_ref, xb_ref, xr_ref)
    spre = mm(xa_ref[...], sgu_ref[:, :half], 1, 1) + mm(xb_ref[...], sgu_ref[:, half:], 1, 1)
    spre_ref[...] = spre
    sgp, sup = spre[:, :unit], spre[:, unit:]
    shid = (sgp * jax.nn.sigmoid(sgp) * sup).astype(BF16)
    shid_ref[...] = shid
    xr = xr_ref[...]
    ready(0, 1)
    gp = mm(xr, wg_ref[...], 1, 1)
    up = mm(xr, wu_ref[...], 1, 1)
    gp_ref[...] = gp
    up_ref[...] = up
    hid = (gp * jax.nn.sigmoid(gp) * up).astype(BF16)
    hid_ref[...] = hid
    ready(2)
    rows = (mm(hid, wd_ref[...], 1, 0) * gate).astype(BF16)
    put_rows(pick, rows, shid, sd_ref, oa_ref, ob_ref)


def backward_kernel(
    place_ref, gate_ref, ca_ref, cb_ref, wg_hbm, wu_hbm, wd_hbm, sgu_ref, sd_ref,
    gp_ref, up_ref, spre_ref,
    oa_ref, ob_ref, cs_ref, ggp_ref, ugp_ref, sgrad_ref, score_ref,
    wg_ref, wu_ref, wd_ref, sems, cr_ref,
):
    ready = fetch((wg_hbm, wu_hbm, wd_hbm), (wg_ref, wu_ref, wd_ref), sems)
    hit, pick, gate = pick_of(place_ref, gate_ref, cr_ref.shape[0])
    half = ca_ref.shape[1]
    unit = sd_ref.shape[0]
    take_rows(pick, ca_ref, cb_ref, cr_ref)
    sgp, sup = spre_ref[:, :unit], spre_ref[:, unit:]
    ssig = jax.nn.sigmoid(sgp)
    sgrad = mm(ca_ref[...], sd_ref[:, :half], 1, 1) + mm(cb_ref[...], sd_ref[:, half:], 1, 1)
    sgg = (sgrad * sup * ssig * (1.0 + sgp * (1.0 - ssig))).astype(BF16)
    sug = (sgrad * sgp * ssig).astype(BF16)
    both = jnp.concatenate([sgg, sug], axis=1)
    sgrad_ref[...] = both
    cr = cr_ref[...]
    cs_ref[...] = (cr.astype(F32) * gate).astype(BF16)
    ready(2)
    raw = mm(cr, wd_ref[...], 1, 1)
    gp, up = gp_ref[...], up_ref[...]
    sig = jax.nn.sigmoid(gp)
    silu = gp * sig
    score = jnp.sum(raw * (silu * up).astype(BF16).astype(F32), axis=1, keepdims=True)
    score_ref[0] = jnp.sum(jnp.where(hit, score, 0.0), axis=0, keepdims=True)
    grad = raw * gate
    ggp = (grad * up * sig * (1.0 + gp * (1.0 - sig))).astype(BF16)
    ugp = (grad * silu).astype(BF16)
    ggp_ref[...] = ggp
    ugp_ref[...] = ugp
    ready(0, 1)
    rows = (mm(ggp, wg_ref[...], 1, 0) + mm(ugp, wu_ref[...], 1, 0)).astype(BF16)
    put_rows(pick, rows, both, sgu_ref, oa_ref, ob_ref)


def spec_rows(rows, width):
    return pl.BlockSpec((rows, width), lambda i: (i, 0))


def spec_info(tok):
    return pl.BlockSpec((1, 1, tok), lambda i: (i, 0, 0))


def spec_whole(array):
    return pl.BlockSpec(array.shape, lambda i: (0,) * array.ndim, pipeline_mode=pl.Buffered(1))


def cost(flops, arrays):
    return pl.CostEstimate(
        flops=int(flops),
        bytes_accessed=int(sum(np.prod(a.shape) * a.dtype.itemsize for a in arrays)),
        transcendentals=0,
    )


def params():
    return pltpu.CompilerParams(
        dimension_semantics=("arbitrary",), vmem_limit_bytes=VMEM_LIMIT
    )


def half_call(name, kernel, place, gate, parts, weights, more, outs, scratch):
    groups, _, tokens = place.shape
    half = parts[0].shape[1]
    ff = weights[0].shape[1]
    hbm = pl.BlockSpec(memory_space=pl.ANY)
    by_group = lambda n: spec_rows(n.shape[0] // groups, n.shape[1])
    args = (place, gate, *parts, *weights, *more)
    rows = outs[2].shape[0]
    unit = weights[4].shape[0]
    flops = 6 * rows * ff * 2 * half + 6 * groups * tokens * unit * 2 * half
    flops += 4 * rows * tokens * half
    return pl.pallas_call(
        kernel,
        grid=(groups,),
        in_specs=[spec_info(tokens)] * 2
        + [by_group(p) for p in parts]
        + [hbm] * 3
        + [spec_whole(w) for w in weights[3:]]
        + [by_group(m) for m in more],
        out_specs=[by_group(o) if len(o.shape) == 2 else spec_info(tokens) for o in outs],
        out_shape=outs,
        scratch_shapes=[pltpu.VMEM(w.shape[1:], BF16) for w in weights[:3]]
        + [pltpu.SemaphoreType.DMA((3,))]
        + scratch,
        compiler_params=params(),
        cost_estimate=cost(4 * flops, list(args) + outs),
        name=name,
    )(*args)


def forward_half(place, gate, parts, weights, rows):
    tokens, half = parts[0].shape
    ff, unit = weights[0].shape[1], weights[4].shape[0]
    shape = jax.ShapeDtypeStruct
    outs = [
        shape((tokens, half), BF16),
        shape((tokens, half), BF16),
        shape((rows, 2 * half), BF16),
        shape((rows, ff), F32),
        shape((rows, ff), F32),
        shape((rows, ff), BF16),
        shape((tokens, 2 * unit), F32),
        shape((tokens, unit), BF16),
    ]
    return half_call("forward_half", forward_kernel, place, gate, parts, weights, (), outs, [])


def backward_half(place, gate, parts, weights, ahead, rows):
    tokens, half = parts[0].shape
    ff, unit = weights[0].shape[1], weights[4].shape[0]
    shape = jax.ShapeDtypeStruct
    outs = [
        shape((tokens, half), BF16),
        shape((tokens, half), BF16),
        shape((rows, 2 * half), BF16),
        shape((rows, ff), BF16),
        shape((rows, ff), BF16),
        shape((tokens, 2 * unit), BF16),
        shape(place.shape, F32),
    ]
    more = (ahead[3], ahead[4], ahead[6])
    scratch = [pltpu.VMEM((rows // place.shape[0], 2 * half), BF16)]
    return half_call(
        "backward_half", backward_kernel, place, gate, parts, weights, more, outs, scratch
    )


def shared_grads_kernel(
    g0_ref, g1_ref, h0_ref, h1_ref, xa0, xa1, xb0, xb1, ca0, ca1, cb0, cb1,
    ga_ref, gb_ref, da_ref, db_ref, gt_ref, ht_ref,
):
    rows = g0_ref.shape[0]

    @pl.when(pl.program_id(0) == 0)
    def _():
        gt_ref[:, :rows] = g0_ref[...].T
        gt_ref[:, rows:] = g1_ref[...].T
        ht_ref[:, :rows] = h0_ref[...].T
        ht_ref[:, rows:] = h1_ref[...].T

    for out, t_ref, one, two in (
        (ga_ref, gt_ref, xa0, xa1),
        (gb_ref, gt_ref, xb0, xb1),
        (da_ref, ht_ref, ca0, ca1),
        (db_ref, ht_ref, cb0, cb1),
    ):
        part = mm(t_ref[:, :rows], one[...], 1, 0) + mm(t_ref[:, rows:], two[...], 1, 0)
        out[...] = part.astype(BF16)


def shared_grads(grads, hiddens, xs, cs):
    rows, half = xs[0].shape
    unit2, unit = grads[0].shape[1], hiddens[0].shape[1]
    tile = min(256, half)
    col = pl.BlockSpec((rows, tile), lambda i: (0, i))
    args = (*grads, *hiddens, *xs, *cs)
    out_shape = [jax.ShapeDtypeStruct((n, half), BF16) for n in (unit2, unit2, unit, unit)]
    return pl.pallas_call(
        shared_grads_kernel,
        grid=(half // tile,),
        in_specs=[spec_whole(a) for a in (*grads, *hiddens)] + [col] * 8,
        out_specs=[pl.BlockSpec((o.shape[0], tile), lambda i: (0, i)) for o in out_shape],
        out_shape=out_shape,
        scratch_shapes=[pltpu.VMEM((unit2, 2 * rows), BF16), pltpu.VMEM((unit, 2 * rows), BF16)],
        compiler_params=params(),
        cost_estimate=cost(8 * rows * half * (unit2 + unit), list(args) + out_shape),
        name="shared_grads",
    )(*args)


def expert_grads_kernel(
    x0_ref, x1_ref, c0_ref, c1_ref, g0_ref, g1_ref, u0_ref, u1_ref, h0_ref, h1_ref,
    wg_ref, wu_ref, wd_ref, gt_ref, ut_ref, ht_ref,
):
    rows = x0_ref.shape[0]

    @pl.when(pl.program_id(0) == 0)
    def _():
        for t_ref, one, two in (
            (gt_ref, g0_ref, g1_ref), (ut_ref, u0_ref, u1_ref), (ht_ref, h0_ref, h1_ref)
        ):
            t_ref[:, :rows] = one[...].T
            t_ref[:, rows:] = two[...].T

    x = jnp.concatenate([x0_ref[...], x1_ref[...]], axis=0)
    c = jnp.concatenate([c0_ref[...], c1_ref[...]], axis=0)
    wg_ref[0] = mm(gt_ref[...], x, 1, 0).astype(BF16)
    wu_ref[0] = mm(ut_ref[...], x, 1, 0).astype(BF16)
    wd_ref[0] = mm(ht_ref[...], c, 1, 0).astype(BF16)


def expert_grads(xr, cs, ggp, ugp, hid):
    rows, width = xr[0].shape
    ff = ggp[0].shape[1]
    tile = min(256, width)
    col = pl.BlockSpec((rows, tile), lambda i: (0, i))
    args = (*xr, *cs, *ggp, *ugp, *hid)
    out_shape = [jax.ShapeDtypeStruct((1, ff, width), BF16)] * 3
    return pl.pallas_call(
        expert_grads_kernel,
        grid=(width // tile,),
        in_specs=[col] * 4 + [spec_whole(a) for a in (*ggp, *ugp, *hid)],
        out_specs=[pl.BlockSpec((1, ff, tile), lambda i: (0, 0, i))] * 3,
        out_shape=out_shape,
        scratch_shapes=[pltpu.VMEM((ff, 2 * rows), BF16)] * 3,
        compiler_params=params(),
        cost_estimate=cost(24 * rows * width * ff, list(args) + out_shape),
        name="expert_grads",
    )(*args)


def local(tokens, expert_ids, gates, w_gate, w_up, w_down, s_gate, s_up, s_down, cotangent):
    tok, width = tokens.shape
    top = expert_ids.shape[1]
    experts, dp = lax.axis_size("expert"), lax.axis_size("dp")
    me, my_dp = lax.axis_index("expert"), lax.axis_index("dp")
    capacity = min(tok, 5 * tok * top // (4 * experts))
    slots = -(-capacity // 16) * 16
    units = s_gate.shape[1] // experts
    share, half = tok // dp, width // 2
    sizes = split_of(experts, dp)
    shares_at = my_dp ^ jnp.arange(dp, dtype=jnp.int32)
    turns = ((3, 1), (1, 3))
    shape = (1,) + sizes[1:] + (share, half)
    flat = lambda parts: [p.reshape(-1, half) for p in parts]
    full = lambda parts: [p.reshape(shape) for p in parts]

    def mine(rows):
        rows = lax.dynamic_slice_in_dim(rows, my_dp * share, share, 0)
        return [rows[:, i * half : (i + 1) * half].reshape(1, 1, 1, 1, share, half) for i in range(2)]

    x1 = [spread(p, sizes, 2) for p in mine(tokens)]
    x2 = [spread(p, sizes, turn[0]) for p, turn in zip(x1, turns)]
    x3 = [spread(p, sizes, turn[1]) for p, turn in zip(x2, turns)]
    own_x = flat(x3)
    other_x = [partner(p, sizes, 0, 1) for p in own_x]
    c1 = [spread(p, sizes, 2) for p in after(mine(cotangent), x1)]

    info = jnp.concatenate([expert_ids.astype(F32), gates], axis=1).T
    info = info.reshape(2 * top, dp, share)[:, shares_at].reshape(1, 1, 1, 1, 2 * top, tok)
    info = spread(spread(after(info, x1), sizes, 2), sizes, 1).reshape(experts // 2, 2 * top, tok)
    info = jnp.stack([info, partner(info, sizes, 0, 1)])

    hit = info[:, :, :top] == me.astype(F32)
    taken = jnp.any(hit, axis=2)
    gate = jnp.sum(jnp.where(hit, info[:, :, top:], 0.0), axis=2)
    before = jnp.triu(jnp.ones((tok, tok), BF16), 1)
    place = mm(taken.astype(BF16).reshape(experts, tok), before, 1, 0).astype(jnp.int32)
    start = slots * (jnp.arange(experts // 2, dtype=jnp.int32) % GROUP)
    place = jnp.where(taken, place.reshape(taken.shape) + start[None, :, None], -1)
    place = place.reshape(2, -1, 1, GROUP * tok)
    gate = gate.reshape(2, -1, 1, GROUP * tok)

    pad = -units % 128
    widen = lambda m: jnp.pad(m, ((0, pad), (0, 0)))
    columns = lambda m: widen(lax.dynamic_slice_in_dim(m, me * units, units, 1).T)
    sgu = jnp.concatenate([columns(s_gate), columns(s_up)], axis=0)
    sd = widen(lax.dynamic_slice_in_dim(s_down, me * units, units, 0))
    weights = (w_gate.swapaxes(1, 2), w_up.swapaxes(1, 2), w_down, sgu, sd)

    rows = experts // 2 * slots
    ahead0 = forward_half(place[0], gate[0], own_x, weights, rows)
    c2 = [spread(p, sizes, turn[0], ahead0[0]) for p, turn in zip(after(c1, x3), turns)]
    ahead1 = forward_half(place[1], gate[1], other_x, weights, rows)
    c3 = [spread(p, sizes, turn[1], ahead1[0]) for p, turn in zip(c2, turns)]
    own_c = flat(c3)
    back0 = backward_half(place[0], gate[0], own_c, weights, ahead0, rows)
    other_c, out_came = after(
        ([partner(p, sizes, 0, 1) for p in own_c], [partner(p, sizes, 0, 1) for p in full(ahead1[:2])]),
        back0[0],
    )
    back1 = backward_half(place[1], gate[1], other_c, weights, ahead1, rows)

    out = [list(t) for t in zip(full(ahead0[:2]), out_came)]
    out = [fold(t, sizes, turn[1], back1[0]) for t, turn in zip(out, turns)]
    ga, gb, da, db = shared_grads(
        [back0[5], back1[5]],
        [ahead0[7], ahead1[7]],
        [own_x[0], other_x[0], own_x[1], other_x[1]],
        [own_c[0], other_c[0], own_c[1], other_c[1]],
    )
    out = [fold(t, sizes, turn[0], ga) for t, turn in zip(out, turns)]
    dx_came = after([partner(p, sizes, 0, 1) for p in full(back1[:2])], ga)
    dx = [list(t) for t in zip(full(back0[:2]), dx_came)]
    grad_wg, grad_wu, grad_wd = expert_grads(
        [ahead0[2], ahead1[2]], [back0[2], back1[2]], [back0[3], back1[3]], [back0[4], back1[4]],
        [ahead0[5], ahead1[5]],
    )
    dx = [fold(t, sizes, turn[1], grad_wg) for t, turn in zip(dx, turns)]
    out = [fold(t, sizes, 2, grad_wg) for t in out]
    moe_out = both_halves(jnp.concatenate([total(t).reshape(share, half) for t in out], axis=1), sizes)
    dx = [fold(t, sizes, turn[0]) for t, turn in zip(dx, turns)]
    dx = [fold(t, sizes, 2) for t in dx]
    token_grads = both_halves(jnp.concatenate([total(t).reshape(share, half) for t in dx], axis=1), sizes)

    unit = units + pad
    both = jnp.concatenate([ga, gb], axis=1)
    grads = jnp.concatenate(
        [both[:units], both[unit : unit + units], jnp.concatenate([da, db], axis=1)[:units]], axis=0
    ).reshape(3 * units, experts, width // experts)
    index = np.arange(experts).reshape(sizes[2], sizes[1], 2).transpose(2, 1, 0).reshape(-1)
    where = jnp.asarray(np.argsort(index), jnp.int32)[me ^ jnp.arange(experts, dtype=jnp.int32)]
    score = jnp.stack([back0[6], back1[6]]).reshape(experts, dp, share)
    score = score[where][:, shares_at].reshape(experts, tok)
    block = grads.shape[2]
    lines = -(-tok // block)
    high = score.astype(BF16)
    low = (score - high.astype(F32)).astype(BF16)
    extra = jnp.pad(jnp.stack([high, low]), ((0, 0), (0, 0), (0, lines * block - tok)))
    extra = extra.reshape(2, experts, lines, block).transpose(0, 2, 1, 3)
    send = jnp.concatenate([grads, extra.reshape(2 * lines, experts, block)], axis=0).transpose(1, 0, 2)
    got = lax.all_to_all(send, "expert", split_axis=0, concat_axis=0, tiled=True)
    grad_sg = got[:, :units].reshape(experts * units, -1).T
    grad_su = got[:, units : 2 * units].reshape(experts * units, -1).T
    grad_sd = got[:, 2 * units : 3 * units].reshape(experts * units, -1)
    scores = got[:, 3 * units :].reshape(experts, 2, lines * block)[:, :, :tok].astype(F32)
    scores = (scores[:, 0] + scores[:, 1]).T
    named = expert_ids[:, :, None] == jnp.arange(experts, dtype=jnp.int32)[None, None, :]
    gate_part = jnp.sum(jnp.where(named, scores[:, None, :], 0.0), axis=2)
    gate_grads = gate_part
    for k in range(1, dp):
        gate_grads = gate_grads + partner(gate_part, sizes, 3, k)

    grad_wg, grad_wu = grad_wg.swapaxes(1, 2), grad_wu.swapaxes(1, 2)
    return (moe_out, token_grads, gate_grads, grad_wg, grad_wu, grad_wd, grad_sg, grad_su, grad_sd)


def solution(mesh):
    row = P("expert", None)
    cols = P("expert", None, "dp")
    return jax.shard_map(
        local,
        mesh=mesh,
        in_specs=(
            row, row, row, cols, cols, P("expert", "dp", None),
            P(None, "dp"), P(None, "dp"), P("dp", None), row,
        ),
        out_specs=(
            row, row, row, cols, cols, P("expert", "dp", None),
            P("expert", "dp"), P("expert", "dp"), P("dp", "expert"),
        ),
        check_vma=False,
    )
```

profile of v0, /device:TPU:8, one launch (start us, length us, event | category | flops | bytes accessed | tf_op | source)
XLA Modules:
  0.0 329.5 jit_solution(524925760505905586)
XLA Ops:
  1.7 3.0 collective-permute-start.4
  17.3 6.4 %collective-permute-done.5 = bf16[1,1,1,1,64,1024]{5,4,3,2,1,0:T(8,128)(2,1)S(1)} collective-permute-done((bf16[1,1,1,1,64,1024]{5,4,3,2,1,0:T(8,128)(2,1)S(1)}, bf16[1,1,1,1,64,1024]{5,4,3,2,1,0:T(8,128)(2,1)S(1)}, u32[]{:S(2)}, u32[]{:S(2)}) %collective-permute-start.5) | collective-permute-done | bytes 131104 | tf_op jit(solution)/shard_map/ppermute | solution.py:34
  25.4 2.5 collective-permute-done.2
  31.9 3.0 collective-permute-start.7
  39.1 3.4 %collective-permute-done.9 = f32[1,1,4,1,12,128]{5,4,3,2,1,0:T(8,128)S(1)} collective-permute-done((f32[1,1,4,1,12,128]{5,4,3,2,1,0:T(8,128)S(1)}, f32[1,1,4,1,12,128]{5,4,3,2,1,0:T(8,128)S(1)}, u32[]{:S(2)}, u32[]{:S(2)}) %collective-permute-start.9) | collective-permute-done | bytes 24608 | tf_op jit(solution)/shard_map/ppermute | solution.py:34
  51.0 2.5 collective-permute-start.15
  53.4 2.4 collective-permute-done.19
  55.9 3.4 %collective-permute-start.16 = (bf16[1,1,1,1,64,1024]{5,4,3,2,1,0:T(8,128)(2,1)S(1)}, bf16[1,1,1,1,64,1024]{5,4,3,2,1,0:T(8,128)(2,1)S(1)}, u32[]{:S(2)}, u32[]{:S(2)}) collective-permute-start(bf16[1,1,1,1,64,1024]{5,4,3,2,1,0:T(8,128)(2,1)S(1)} %get-tuple-element.105), channel_id=1, source_target_pairs={{0,8},{1,9},{2,10},{3,11},{4,12},{5,13},{6,14},{7,15},{8,0},{9,1},... | collective-permute-start | bytes 393224 | tf_op jit(solution)/shard_map/ppermute | solution.py:34
  59.3 6.0 %collective-permute-done.20 = bf16[1,1,1,1,64,1024]{5,4,3,2,1,0:T(8,128)(2,1)S(1)} collective-permute-done((bf16[1,1,1,1,64,1024]{5,4,3,2,1,0:T(8,128)(2,1)S(1)}, bf16[1,1,1,1,64,1024]{5,4,3,2,1,0:T(8,128)(2,1)S(1)}, u32[]{:S(2)}, u32[]{:S(2)}) %collective-permute-start.20) | collective-permute-done | bytes 131104 | tf_op jit(solution)/shard_map/ppermute | solution.py:34
  67.4 2.9 collective-permute-done.17
  76.0 17.3 %forward_half.2 = (bf16[1024,1024]{1,0:T(8,128)(2,1)}, bf16[1024,1024]{1,0:T(8,128)(2,1)}, bf16[512,2048]{1,0:T(8,128)(2,1)}, f32[512,704]{1,0:T(8,128)}, f32[51...) custom-call(s32[2,1,512]{2,1,0:T(1,128)} %bitcast.136, ...), custom_call_target="tpu_custom_call" | custom-call | flops 28454158336 | bytes 25632768 | tf_op jit(solution)/shard_map/forward_half/pallas_call | solution.py:214
  96.6 17.3 %forward_half.3 = (bf16[1024,1024]{1,0:T(8,128)(2,1)}, bf16[1024,1024]{1,0:T(8,128)(2,1)}, bf16[512,2048]{1,0:T(8,128)(2,1)}, f32[512,704]{1,0:T(8,128)}, f32[51...) custom-call(s32[2,1,512]{2,1,0:T(1,128)} %bitcast.132, ...), custom_call_target="tpu_custom_call" | custom-call | flops 28454158336 | bytes 25632768 | tf_op jit(solution)/shard_map/forward_half/pallas_call | solution.py:214
  113.9 4.4 %collective-permute-done.27 = bf16[1,2,4,1,64,1024]{5,4,3,2,1,0:T(8,128)(2,1)S(1)} collective-permute-done((bf16[1,2,4,1,64,1024]{5,4,3,2,1,0:T(8,128)(2,1)S(1)}, bf16[1,2,4,1,64,1024]{5,4,3,2,1,0:T(8,128)(2,1)S(1)}, u32[]{:S(2)}, u32[]{:S(2)}) %collective-permute-start.27) | collective-permute-done | bytes 1048608 | tf_op jit(solution)/shard_map/ppermute | solution.py:34
  123.5 19.6 %backward_half.2 = (bf16[1024,1024]{1,0:T(8,128)(2,1)}, bf16[1024,1024]{1,0:T(8,128)(2,1)}, bf16[512,2048]{1,0:T(8,128)(2,1)}, bf16[512,704]{1,0:T(8,128)(2,1)},...) custom-call(s32[2,1,512]{2,1,0:T(1,128)} %bitcast.137, f32[2,1,512]{2,1,0:T(1,128)} %bitcast.139, ...), custom_call_target="tpu_custom_call" | custom-call | flops 28454158336 | bytes 26619904 | tf_op jit(solution)/shard_map/backward_half/pallas_call | solution.py:214
  144.3 19.5 %backward_half.3 = (bf16[1024,1024]{1,0:T(8,128)(2,1)}, bf16[1024,1024]{1,0:T(8,128)(2,1)}, bf16[512,2048]{1,0:T(8,128)(2,1)}, bf16[512,704]{1,0:T(8,128)(2,1)},...) custom-call(s32[2,1,512]{2,1,0:T(1,128)} %bitcast.133, f32[2,1,512]{2,1,0:T(1,128)} %bitcast.135, ...), custom_call_target="tpu_custom_call" | custom-call | flops 28454158336 | bytes 26619904 | tf_op jit(solution)/shard_map/backward_half/pallas_call | solution.py:214
  164.4 2.7 add_convert_fusion.3
  170.3 10.4 %shared_grads.1 = (bf16[256,1024]{1,0:T(8,128)(2,1)}, bf16[256,1024]{1,0:T(8,128)(2,1)}, bf16[128,1024]{1,0:T(8,128)(2,1)}, bf16[128,1024]{1,0:T(8,128)(2,1)}) custom-call(bf16[1024,256]{1,0:T(8,128)(2,1)} %get-tuple-element.133.g0_ref, bf16[1024,256]{1,0:T(8,128)(2,1)} %get-tuple-element.134.g1_ref, bf16[1024,128]{1,0:T(8,128)(2,1)} %get-tuple-element.135.h0_ref, ...), custom_call_target="tpu_custom_call" | custom-call | flops 3221225472 | bytes 19922944 | tf_op jit(solution)/shard_map/shared_grads/pallas_call | solution.py:300
  184.4 8.2 %collective-permute-done.31 = bf16[1,1,4,2,64,1024]{5,4,3,2,1,0:T(8,128)(2,1)} collective-permute-done((bf16[1,1,4,2,64,1024]{5,4,3,2,1,0:T(8,128)(2,1)}, bf16[1,1,4,2,64,1024]{5,4,3,2,1,0:T(8,128)(2,1)}, u32[]{:S(2)}, u32[]{:S(2)}) %collective-permute-start.31) | collective-permute-done | bytes 1048608 | tf_op jit(solution)/shard_map/ppermute | solution.py:34
  192.6 2.4 add_convert_fusion.7
  199.3 6.1 %all-to-all-start = ((bf16[16,266,128]{2,1,0:T(8,128)(2,1)}), bf16[16,266,128]{2,1,0:T(8,128)(2,1)S(1)}, u32[]{:S(2)}, u32[]{:S(2)}) async-start(bf16[16,266,128]{2,1,0:T(8,128)(2,1)} %maximum_bitcast_fusion), calls=%async_computation | async-start | bytes 2228224 | tf_op jit(solution)/shard_map/all_to_all | solution.py:454
  205.3 3.0 collective-permute-done.32
  215.3 2.4 add_convert_fusion.17
  217.7 4.1 %collective-permute-start.38 = (bf16[1,1,1,1,64,1024]{5,4,3,2,1,0:T(8,128)(2,1)}, bf16[1,1,1,1,64,1024]{5,4,3,2,1,0:T(8,128)(2,1)S(1)}, u32[]{:S(2)}, u32[]{:S(2)}) collective-permute-start(bf16[1,1,1,1,64,1024]{5,4,3,2,1,0:T(8,128)(2,1)} %get-tuple-element.221), channel_id=1, source_target_pairs={{0,4},{1,5},{2,6},{3,7},{4,0},{5,1},{6,2},{7,3},{8,12},{9,13},{10,... | collective-permute-start | bytes 393224 | tf_op jit(solution)/shard_map/ppermute | solution.py:34
  228.1 2.8 collective-permute-start.40
  230.8 13.7 %collective-permute-done.34 = bf16[1,1,1,1,64,1024]{5,4,3,2,1,0:T(8,128)(2,1)S(1)} collective-permute-done((bf16[1,1,1,1,64,1024]{5,4,3,2,1,0:T(8,128)(2,1)S(1)}, bf16[1,1,1,1,64,1024]{5,4,3,2,1,0:T(8,128)(2,1)S(1)}, u32[]{:S(2)}, u32[]{:S(2)}) %collective-permute-start.34) | collective-permute-done | bytes 131104 | tf_op jit(solution)/shard_map/ppermute | solution.py:34
  246.0 3.3 %collective-permute-done.35 = bf16[1,1,1,1,64,1024]{5,4,3,2,1,0:T(8,128)(2,1)S(1)} collective-permute-done((bf16[1,1,1,1,64,1024]{5,4,3,2,1,0:T(8,128)(2,1)S(1)}, bf16[1,1,1,1,64,1024]{5,4,3,2,1,0:T(8,128)(2,1)S(1)}, u32[]{:S(2)}, u32[]{:S(2)}) %collective-permute-start.35) | collective-permute-done | bytes 131104 | tf_op jit(solution)/shard_map/ppermute | solution.py:34
  250.4 15.9 %expert_grads.1 = (bf16[1,704,2048]{2,1,0:T(8,128)(2,1)}, bf16[1,704,2048]{2,1,0:T(8,128)(2,1)}, bf16[1,704,2048]{2,1,0:T(8,128)(2,1)}) custom-call(bf16[512,2048]{1,0:T(8,128)(2,1)} %get-tuple-element.139.x0_ref, bf16[512,2048]{1,0:T(8,128)(2,1)} %get-tuple-element.140.x1_ref, bf16[512,2048]{1,0:T(8,128)(2,1)} %get-tuple-element.141.c0_ref, ...), custom_call_target="tpu_custom_call" | custom-call | flops 17716740096 | bytes 21364736 | tf_op jit(solution)/shard_map/expert_grads/pallas_call | solution.py:341
  281.9 2.4 gather_fusion.1
  284.3 6.3 %collective-permute-done.45 = bf16[1,1,4,1,64,1024]{5,4,3,2,1,0:T(8,128)(2,1)} collective-permute-done((bf16[1,1,4,1,64,1024]{5,4,3,2,1,0:T(8,128)(2,1)}, bf16[1,1,4,1,64,1024]{5,4,3,2,1,0:T(8,128)(2,1)}, u32[]{:S(2)}, u32[]{:S(2)}) %collective-permute-start.45) | collective-permute-done | bytes 524320 | tf_op jit(solution)/shard_map/ppermute | solution.py:34
  301.5 10.7 %collective-permute-done.48 = bf16[1,1,1,1,64,1024]{5,4,3,2,1,0:T(8,128)(2,1)S(1)} collective-permute-done((bf16[1,1,1,1,64,1024]{5,4,3,2,1,0:T(8,128)(2,1)S(1)}, bf16[1,1,1,1,64,1024]{5,4,3,2,1,0:T(8,128)(2,1)S(1)}, u32[]{:S(2)}, u32[]{:S(2)}) %collective-permute-start.48) | collective-permute-done | bytes 131104 | tf_op jit(solution)/shard_map/ppermute | solution.py:34
  313.4 3.6 %collective-permute-done.53 = bf16[1,1,1,1,64,1024]{5,4,3,2,1,0:T(8,128)(2,1)S(1)} collective-permute-done((bf16[1,1,1,1,64,1024]{5,4,3,2,1,0:T(8,128)(2,1)S(1)}, bf16[1,1,1,1,64,1024]{5,4,3,2,1,0:T(8,128)(2,1)S(1)}, u32[]{:S(2)}, u32[]{:S(2)}) %collective-permute-start.53) | collective-permute-done | bytes 131104 | tf_op jit(solution)/shard_map/ppermute | solution.py:34
  324.3 2.8 collective-permute-done.55
  (210 shorter events, 113.5 us)
Async XLA Ops:
  4.7 18.9 %collective-permute-start.5 = (bf16[1,1,1,1,64,1024]{5,4,3,2,1,0:T(8,128)(2,1)S(1)}, bf16[1,1,1,1,64,1024]{5,4,3,2,1,0:T(8,128)(2,1)S(1)}, u32[]{:S(2)}, u32[]{:S(2)}) collective-permute-start(bf16[1,1,1,1,64,1024]{5,4,3,2,1,0:T(8,128)(2,1)S(1)} %get-tuple-element.229), channel_id=1, source_target_pairs={{0,12},{1,13},{2,14},{3,15},{4,8},{5,9},{6,10},{7,11},{8,4},{9,5},... | collective-permute-start | bytes 393224 | tf_op jit(solution)/shard_map/ppermute | solution.py:34
  5.2 18.4 %collective-permute-start = (bf16[1,1,1,1,64,1024]{5,4,3,2,1,0:T(8,128)(2,1)S(1)}, bf16[1,1,1,1,64,1024]{5,4,3,2,1,0:T(8,128)(2,1)S(1)}, u32[]{:S(2)}, u32[]{:S(2)}) collective-permute-start(bf16[1,1,1,1,64,1024]{5,4,3,2,1,0:T(8,128)(2,1)S(1)} %get-tuple-element.230), channel_id=1, source_target_pairs={{0,4},{1,5},{2,6},{3,7},{4,0},{5,1},{6,2},{7,3},{8,12},{9,13},{10,... | collective-permute-start | bytes 393224 | tf_op jit(solution)/shard_map/ppermute | solution.py:34
  6.3 19.1 %collective-permute-start.1 = (bf16[1,1,1,1,64,1024]{5,4,3,2,1,0:T(8,128)(2,1)S(1)}, bf16[1,1,1,1,64,1024]{5,4,3,2,1,0:T(8,128)(2,1)S(1)}, u32[]{:S(2)}, u32[]{:S(2)}) collective-permute-start(bf16[1,1,1,1,64,1024]{5,4,3,2,1,0:T(8,128)(2,1)S(1)} %get-tuple-element.230), channel_id=1, source_target_pairs={{0,8},{1,9},{2,10},{3,11},{4,12},{5,13},{6,14},{7,15},{8,0},{9,1},... | collective-permute-start | bytes 393224 | tf_op jit(solution)/shard_map/ppermute | solution.py:34
  28.7 18.3 %collective-permute-start.13 = (bf16[1,1,4,1,64,1024]{5,4,3,2,1,0:T(8,128)(2,1)}, bf16[1,1,4,1,64,1024]{5,4,3,2,1,0:T(8,128)(2,1)S(1)}, u32[]{:S(2)}, u32[]{:S(2)}) collective-permute-start(bf16[1,1,4,1,64,1024]{5,4,3,2,1,0:T(8,128)(2,1)} %pad_maximum_fusion.8), channel_id=1, source_target_pairs={{0,2},{1,3},{2,0},{3,1},{4,6},{5,7},{6,4},{7,5},{8,10},{9,11},{10,... | collective-permute-start | bytes 1572872 | tf_op jit(solution)/shard_map/ppermute | solution.py:34
  46.3 19.0 %collective-permute-start.20 = (bf16[1,1,1,1,64,1024]{5,4,3,2,1,0:T(8,128)(2,1)S(1)}, bf16[1,1,1,1,64,1024]{5,4,3,2,1,0:T(8,128)(2,1)S(1)}, u32[]{:S(2)}, u32[]{:S(2)}) collective-permute-start(bf16[1,1,1,1,64,1024]{5,4,3,2,1,0:T(8,128)(2,1)S(1)} %get-tuple-element.109), channel_id=1, source_target_pairs={{0,12},{1,13},{2,14},{3,15},{4,8},{5,9},{6,10},{7,11},{8,4},{9,5},... | collective-permute-start | bytes 393224 | tf_op jit(solution)/shard_map/ppermute | solution.py:34
  47.1 24.8 %collective-permute-start.14 = (bf16[1,2,4,1,64,1024]{5,4,3,2,1,0:T(8,128)(2,1)S(1)}, bf16[1,2,4,1,64,1024]{5,4,3,2,1,0:T(8,128)(2,1)S(1)}, u32[]{:S(2)}, u32[]{:S(2)}) collective-permute-start(bf16[1,2,4,1,64,1024]{5,4,3,2,1,0:T(8,128)(2,1)S(1)} %pad_maximum_fusion.6), channel_id=1, source_target_pairs={{0,16},{16,0},{1,17},{17,1},{2,18},{18,2},{3,19},{19,3},{4,20},{20... | collective-permute-start | bytes 3145736 | tf_op jit(solution)/shard_map/ppermute | solution.py:34
  48.2 24.8 %collective-permute-start.12 = (bf16[1,1,4,2,64,1024]{5,4,3,2,1,0:T(8,128)(2,1)S(1)}, bf16[1,1,4,2,64,1024]{5,4,3,2,1,0:T(8,128)(2,1)S(1)}, u32[]{:S(2)}, u32[]{:S(2)}) collective-permute-start(bf16[1,1,4,2,64,1024]{5,4,3,2,1,0:T(8,128)(2,1)S(1)} %pad_maximum_fusion.5), channel_id=1, source_target_pairs={{0,2},{1,3},{2,0},{3,1},{4,6},{5,7},{6,4},{7,5},{8,10},{9,11},{10,... | collective-permute-start | bytes 3145736 | tf_op jit(solution)/shard_map/ppermute | solution.py:34
  73.3 20.1 %collective-permute-start.26 = (bf16[1,1,4,1,64,1024]{5,4,3,2,1,0:T(8,128)(2,1)S(1)}, bf16[1,1,4,1,64,1024]{5,4,3,2,1,0:T(8,128)(2,1)S(1)}, u32[]{:S(2)}, u32[]{:S(2)}) collective-permute-start(bf16[1,1,4,1,64,1024]{5,4,3,2,1,0:T(8,128)(2,1)S(1)} %pad_maximum_fusion.10), channel_id=1, source_target_pairs={{0,2},{1,3},{2,0},{3,1},{4,6},{5,7},{6,4},{7,5},{8,10},{9,11},{10,... | collective-permute-start | bytes 1572872 | tf_op jit(solution)/shard_map/ppermute | solution.py:34
  74.9 21.8 %collective-permute-start.24 = (bf16[1024,1024]{1,0:T(8,128)(2,1)S(1)}, bf16[1024,1024]{1,0:T(8,128)(2,1)}, u32[]{:S(2)}, u32[]{:S(2)}) collective-permute-start(bf16[1024,1024]{1,0:T(8,128)(2,1)S(1)} %bitcast.89), channel_id=1, source_target_pairs={{0,1},{1,0},{2,3},{3,2},{4,5},{5,4},{6,7},{7,6},{8,9},{9,8},{10,11... | collective-permute-start | bytes 6291464 | tf_op jit(solution)/shard_map/ppermute | solution.py:34
  74.9 21.8 %collective-permute-start.23 = (bf16[1024,1024]{1,0:T(8,128)(2,1)S(1)}, bf16[1024,1024]{1,0:T(8,128)(2,1)}, u32[]{:S(2)}, u32[]{:S(2)}) collective-permute-start(bf16[1024,1024]{1,0:T(8,128)(2,1)S(1)} %bitcast.92), channel_id=1, source_target_pairs={{0,1},{1,0},{2,3},{3,2},{4,5},{5,4},{6,7},{7,6},{8,9},{9,8},{10,11... | collective-permute-start | bytes 6291464 | tf_op jit(solution)/shard_map/ppermute | solution.py:34
  75.4 19.6 %collective-permute-start.21 = (bf16[1,1,4,1,64,1024]{5,4,3,2,1,0:T(8,128)(2,1)S(1)}, bf16[1,1,4,1,64,1024]{5,4,3,2,1,0:T(8,128)(2,1)}, u32[]{:S(2)}, u32[]{:S(2)}) collective-permute-start(bf16[1,1,4,1,64,1024]{5,4,3,2,1,0:T(8,128)(2,1)S(1)} %pad_maximum_fusion.9), channel_id=1, source_target_pairs={{0,16},{16,0},{1,17},{17,1},{2,18},{18,2},{3,19},{19,3},{4,20},{20... | collective-permute-start | bytes 1572872 | tf_op jit(solution)/shard_map/ppermute | solution.py:34
  93.4 24.9 %collective-permute-start.27 = (bf16[1,2,4,1,64,1024]{5,4,3,2,1,0:T(8,128)(2,1)S(1)}, bf16[1,2,4,1,64,1024]{5,4,3,2,1,0:T(8,128)(2,1)S(1)}, u32[]{:S(2)}, u32[]{:S(2)}) collective-permute-start(bf16[1,2,4,1,64,1024]{5,4,3,2,1,0:T(8,128)(2,1)S(1)} %constant_dynamic-update-slice_fusion.6), channel_id=1, source_target_pairs={{0,16},{16,0},{1,17},{17,1},{2,18},{18,2},{3,19},{19,3},{4,20},{20... | collective-permute-start | bytes 3145736 | tf_op jit(solution)/shard_map/ppermute | solution.py:34
  96.1 24.7 %collective-permute-start.22 = (bf16[1,1,4,2,64,1024]{5,4,3,2,1,0:T(8,128)(2,1)S(1)}, bf16[1,1,4,2,64,1024]{5,4,3,2,1,0:T(8,128)(2,1)}, u32[]{:S(2)}, u32[]{:S(2)}) collective-permute-start(bf16[1,1,4,2,64,1024]{5,4,3,2,1,0:T(8,128)(2,1)S(1)} %constant_dynamic-update-slice_fusion.4), channel_id=1, source_target_pairs={{0,2},{1,3},{2,0},{3,1},{4,6},{5,7},{6,4},{7,5},{8,10},{9,11},{10,... | collective-permute-start | bytes 3145736 | tf_op jit(solution)/shard_map/ppermute | solution.py:34
  122.2 20.9 %collective-permute-start.28 = (bf16[1024,1024]{1,0:T(8,128)(2,1)S(1)}, bf16[1024,1024]{1,0:T(8,128)(2,1)S(1)}, u32[]{:S(2)}, u32[]{:S(2)}) collective-permute-start(bf16[1024,1024]{1,0:T(8,128)(2,1)S(1)} %bitcast.95), channel_id=1, source_target_pairs={{0,1},{1,0},{2,3},{3,2},{4,5},{5,4},{6,7},{7,6},{8,9},{9,8},{10,11... | collective-permute-start | bytes 6291464 | tf_op jit(solution)/shard_map/ppermute | solution.py:34
  122.2 20.8 %collective-permute-start.25 = (bf16[1024,1024]{1,0:T(8,128)(2,1)S(1)}, bf16[1024,1024]{1,0:T(8,128)(2,1)}, u32[]{:S(2)}, u32[]{:S(2)}) collective-permute-start(bf16[1024,1024]{1,0:T(8,128)(2,1)S(1)} %bitcast.98), channel_id=1, source_target_pairs={{0,1},{1,0},{2,3},{3,2},{4,5},{5,4},{6,7},{7,6},{8,9},{9,8},{10,11... | collective-permute-start | bytes 6291464 | tf_op jit(solution)/shard_map/ppermute | solution.py:34
  122.7 20.3 %collective-permute-start.29 = (bf16[1,2,4,2,64,1024]{5,4,3,2,1,0:T(8,128)(2,1)}, bf16[1,2,4,2,64,1024]{5,4,3,2,1,0:T(8,128)(2,1)}, u32[]{:S(2)}, u32[]{:S(2)}) collective-permute-start(bf16[1,2,4,2,64,1024]{5,4,3,2,1,0:T(8,128)(2,1)} %bitcast.25), channel_id=1, source_target_pairs={{0,1},{1,0},{2,3},{3,2},{4,5},{5,4},{6,7},{7,6},{8,9},{9,8},{10,11... | collective-permute-start | bytes 6291464 | tf_op jit(solution)/shard_map/ppermute | solution.py:34
  122.8 20.3 %collective-permute-start.30 = (bf16[1,2,4,2,64,1024]{5,4,3,2,1,0:T(8,128)(2,1)}, bf16[1,2,4,2,64,1024]{5,4,3,2,1,0:T(8,128)(2,1)}, u32[]{:S(2)}, u32[]{:S(2)}) collective-permute-start(bf16[1,2,4,2,64,1024]{5,4,3,2,1,0:T(8,128)(2,1)} %bitcast.26), channel_id=1, source_target_pairs={{0,1},{1,0},{2,3},{3,2},{4,5},{5,4},{6,7},{7,6},{8,9},{9,8},{10,11... | collective-permute-start | bytes 6291464 | tf_op jit(solution)/shard_map/ppermute | solution.py:34
  163.8 53.9 %collective-permute-start.42 = (bf16[1,2,4,2,64,1024]{5,4,3,2,1,0:T(8,128)(2,1)}, bf16[1,2,4,2,64,1024]{5,4,3,2,1,0:T(8,128)(2,1)}, u32[]{:S(2)}, u32[]{:S(2)}) collective-permute-start(bf16[1,2,4,2,64,1024]{5,4,3,2,1,0:T(8,128)(2,1)} %bitcast.151), channel_id=1, source_target_pairs={{0,1},{1,0},{2,3},{3,2},{4,5},{5,4},{6,7},{7,6},{8,9},{9,8},{10,11... | collective-permute-start | bytes 6291464 | tf_op jit(solution)/shard_map/ppermute | solution.py:34
  163.9 58.0 %collective-permute-start.43 = (bf16[1,2,4,2,64,1024]{5,4,3,2,1,0:T(8,128)(2,1)}, bf16[1,2,4,2,64,1024]{5,4,3,2,1,0:T(8,128)(2,1)}, u32[]{:S(2)}, u32[]{:S(2)}) collective-permute-start(bf16[1,2,4,2,64,1024]{5,4,3,2,1,0:T(8,128)(2,1)} %bitcast.150), channel_id=1, source_target_pairs={{0,1},{1,0},{2,3},{3,2},{4,5},{5,4},{6,7},{7,6},{8,9},{9,8},{10,11... | collective-permute-start | bytes 6291464 | tf_op jit(solution)/shard_map/ppermute | solution.py:34
  167.1 25.4 %collective-permute-start.31 = (bf16[1,1,4,2,64,1024]{5,4,3,2,1,0:T(8,128)(2,1)}, bf16[1,1,4,2,64,1024]{5,4,3,2,1,0:T(8,128)(2,1)}, u32[]{:S(2)}, u32[]{:S(2)}) collective-permute-start(bf16[1,1,4,2,64,1024]{5,4,3,2,1,0:T(8,128)(2,1)} %add_convert_fusion.3), channel_id=1, source_target_pairs={{0,2},{1,3},{2,0},{3,1},{4,6},{5,7},{6,4},{7,5},{8,10},{9,11},{10,... | collective-permute-start | bytes 3145736 | tf_op jit(solution)/shard_map/ppermute | solution.py:34
  169.2 26.3 %collective-permute-start.36 = (bf16[1,2,4,1,64,1024]{5,4,3,2,1,0:T(8,128)(2,1)S(1)}, bf16[1,2,4,1,64,1024]{5,4,3,2,1,0:T(8,128)(2,1)}, u32[]{:S(2)}, u32[]{:S(2)}) collective-permute-start(bf16[1,2,4,1,64,1024]{5,4,3,2,1,0:T(8,128)(2,1)S(1)} %add_convert_fusion.2), channel_id=1, source_target_pairs={{0,16},{16,0},{1,17},{17,1},{2,18},{18,2},{3,19},{19,3},{4,20},{20... | collective-permute-start | bytes 3145736 | tf_op jit(solution)/shard_map/ppermute | solution.py:34
  199.3 85.1 %all-to-all-start = ((bf16[16,266,128]{2,1,0:T(8,128)(2,1)}), bf16[16,266,128]{2,1,0:T(8,128)(2,1)S(1)}, u32[]{:S(2)}, u32[]{:S(2)}) async-start(bf16[16,266,128]{2,1,0:T(8,128)(2,1)} %maximum_bitcast_fusion), calls=%async_computation | async-start | bytes 2228224 | tf_op jit(solution)/shard_map/all_to_all | solution.py:454
  210.0 18.0 %collective-permute-start.33 = (bf16[1,1,1,1,64,1024]{5,4,3,2,1,0:T(8,128)(2,1)S(1)}, bf16[1,1,1,1,64,1024]{5,4,3,2,1,0:T(8,128)(2,1)S(1)}, u32[]{:S(2)}, u32[]{:S(2)}) collective-permute-start(bf16[1,1,1,1,64,1024]{5,4,3,2,1,0:T(8,128)(2,1)S(1)} %get-tuple-element.218), channel_id=1, source_target_pairs={{0,4},{1,5},{2,6},{3,7},{4,0},{5,1},{6,2},{7,3},{8,12},{9,13},{10,... | collective-permute-start | bytes 393224 | tf_op jit(solution)/shard_map/ppermute | solution.py:34
  211.6 33.0 %collective-permute-start.34 = (bf16[1,1,1,1,64,1024]{5,4,3,2,1,0:T(8,128)(2,1)S(1)}, bf16[1,1,1,1,64,1024]{5,4,3,2,1,0:T(8,128)(2,1)S(1)}, u32[]{:S(2)}, u32[]{:S(2)}) collective-permute-start(bf16[1,1,1,1,64,1024]{5,4,3,2,1,0:T(8,128)(2,1)S(1)} %get-tuple-element.217), channel_id=1, source_target_pairs={{0,8},{1,9},{2,10},{3,11},{4,12},{5,13},{6,14},{7,15},{8,0},{9,1},... | collective-permute-start | bytes 393224 | tf_op jit(solution)/shard_map/ppermute | solution.py:34
  214.1 35.3 %collective-permute-start.35 = (bf16[1,1,1,1,64,1024]{5,4,3,2,1,0:T(8,128)(2,1)S(1)}, bf16[1,1,1,1,64,1024]{5,4,3,2,1,0:T(8,128)(2,1)S(1)}, u32[]{:S(2)}, u32[]{:S(2)}) collective-permute-start(bf16[1,1,1,1,64,1024]{5,4,3,2,1,0:T(8,128)(2,1)S(1)} %get-tuple-element.216), channel_id=1, source_target_pairs={{0,12},{1,13},{2,14},{3,15},{4,8},{5,9},{6,10},{7,11},{8,4},{9,5},... | collective-permute-start | bytes 393224 | tf_op jit(solution)/shard_map/ppermute | solution.py:34
  217.7 48.6 %collective-permute-start.38 = (bf16[1,1,1,1,64,1024]{5,4,3,2,1,0:T(8,128)(2,1)}, bf16[1,1,1,1,64,1024]{5,4,3,2,1,0:T(8,128)(2,1)S(1)}, u32[]{:S(2)}, u32[]{:S(2)}) collective-permute-start(bf16[1,1,1,1,64,1024]{5,4,3,2,1,0:T(8,128)(2,1)} %get-tuple-element.221), channel_id=1, source_target_pairs={{0,4},{1,5},{2,6},{3,7},{4,0},{5,1},{6,2},{7,3},{8,12},{9,13},{10,... | collective-permute-start | bytes 393224 | tf_op jit(solution)/shard_map/ppermute | solution.py:34
  221.9 44.5 %collective-permute-start.39 = (bf16[1,1,1,1,64,1024]{5,4,3,2,1,0:T(8,128)(2,1)}, bf16[1,1,1,1,64,1024]{5,4,3,2,1,0:T(8,128)(2,1)S(1)}, u32[]{:S(2)}, u32[]{:S(2)}) collective-permute-start(bf16[1,1,1,1,64,1024]{5,4,3,2,1,0:T(8,128)(2,1)} %get-tuple-element.220), channel_id=1, source_target_pairs={{0,8},{1,9},{2,10},{3,11},{4,12},{5,13},{6,14},{7,15},{8,0},{9,1},... | collective-permute-start | bytes 393224 | tf_op jit(solution)/shard_map/ppermute | solution.py:34
  228.1 38.3 %collective-permute-start.40 = (bf16[1,1,1,1,64,1024]{5,4,3,2,1,0:T(8,128)(2,1)S(1)}, bf16[1,1,1,1,64,1024]{5,4,3,2,1,0:T(8,128)(2,1)}, u32[]{:S(2)}, u32[]{:S(2)}) collective-permute-start(bf16[1,1,1,1,64,1024]{5,4,3,2,1,0:T(8,128)(2,1)S(1)} %get-tuple-element.219), channel_id=1, source_target_pairs={{0,12},{1,13},{2,14},{3,15},{4,8},{5,9},{6,10},{7,11},{8,4},{9,5},... | collective-permute-start | bytes 393224 | tf_op jit(solution)/shard_map/ppermute | solution.py:34
  244.6 25.4 %collective-permute-start.44 = (bf16[1,1,4,2,64,1024]{5,4,3,2,1,0:T(8,128)(2,1)S(1)}, bf16[1,1,4,2,64,1024]{5,4,3,2,1,0:T(8,128)(2,1)}, u32[]{:S(2)}, u32[]{:S(2)}) collective-permute-start(bf16[1,1,4,2,64,1024]{5,4,3,2,1,0:T(8,128)(2,1)S(1)} %add_convert_fusion.1), channel_id=1, source_target_pairs={{0,2},{1,3},{2,0},{3,1},{4,6},{5,7},{6,4},{7,5},{8,10},{9,11},{10,... | collective-permute-start | bytes 3145736 | tf_op jit(solution)/shard_map/ppermute | solution.py:34
  249.4 26.2 %collective-permute-start.49 = (bf16[1,2,4,1,64,1024]{5,4,3,2,1,0:T(8,128)(2,1)S(1)}, bf16[1,2,4,1,64,1024]{5,4,3,2,1,0:T(8,128)(2,1)}, u32[]{:S(2)}, u32[]{:S(2)}) collective-permute-start(bf16[1,2,4,1,64,1024]{5,4,3,2,1,0:T(8,128)(2,1)S(1)} %add_convert_fusion), channel_id=1, source_target_pairs={{0,16},{16,0},{1,17},{17,1},{2,18},{18,2},{3,19},{19,3},{4,20},{20... | collective-permute-start | bytes 3145736 | tf_op jit(solution)/shard_map/ppermute | solution.py:34
  272.3 18.3 %collective-permute-start.45 = (bf16[1,1,4,1,64,1024]{5,4,3,2,1,0:T(8,128)(2,1)}, bf16[1,1,4,1,64,1024]{5,4,3,2,1,0:T(8,128)(2,1)}, u32[]{:S(2)}, u32[]{:S(2)}) collective-permute-start(bf16[1,1,4,1,64,1024]{5,4,3,2,1,0:T(8,128)(2,1)} %add_convert_fusion.5), channel_id=1, source_target_pairs={{0,16},{16,0},{1,17},{17,1},{2,18},{18,2},{3,19},{19,3},{4,20},{20... | collective-permute-start | bytes 1572872 | tf_op jit(solution)/shard_map/ppermute | solution.py:34
  277.8 18.1 %collective-permute-start.50 = (bf16[1,1,4,1,64,1024]{5,4,3,2,1,0:T(8,128)(2,1)}, bf16[1,1,4,1,64,1024]{5,4,3,2,1,0:T(8,128)(2,1)}, u32[]{:S(2)}, u32[]{:S(2)}) collective-permute-start(bf16[1,1,4,1,64,1024]{5,4,3,2,1,0:T(8,128)(2,1)} %add_convert_fusion.4), channel_id=1, source_target_pairs={{0,2},{1,3},{2,0},{3,1},{4,6},{5,7},{6,4},{7,5},{8,10},{9,11},{10,... | collective-permute-start | bytes 1572872 | tf_op jit(solution)/shard_map/ppermute | solution.py:34
  (41 other events, 431.2 us)
where the time goes:
time: 334 us; the launch traced here: 330 us
  Pallas kernels  100 us (30%)
  waiting for transfers between devices  96.6 us (29%)
  starting transfers between devices  71.6 us (21%)
  other arithmetic  37.6 us (11%)
  local copies, waits for them, and re-layouts  22 us (7%)
    ppermute x56, waiting for transfers between devices, partner(): lax.ppermute(array, axis, [(i, i ^ mask) for i in range(lax.axis_size(axi...  96.6 us
    pallas_call x4, Pallas kernels, half_call(): pl.pallas_call(kernel, grid=(groups,), in_specs=[spec_info(tokens)] * 2 +...  73.6 us
    ppermute x56, starting transfers between devices, partner(): lax.ppermute(array, axis, [(i, i ^ mask) for i in range(lax.axis_size(axi...  65.5 us
    convert_element_type x12, other arithmetic, total(): return out.astype(BF16)  23.5 us
    pallas_call x1, Pallas kernels, expert_grads(): pl.pallas_call(expert_grads_kernel, grid=(width // tile,), in_specs=[col]...  15.9 us
    pallas_call x1, Pallas kernels, shared_grads(): pl.pallas_call(shared_grads_kernel, grid=(half // tile,), in_specs=[spec_...  10.4 us
  transfers between devices with their start and end apart: 57, of which 28 were waited for; matrix products, arithmetic and copies ran while one was open for 15% of the time, Pallas kernels for 24%

commit v1 on v0

--- a/solution.py
+++ b/solution.py
@@ -50,10 +50,13 @@
     return out.astype(BF16)
 
 
-def fold(terms, sizes, dim, *earlier):
+def parts_for(terms, sizes, dim):
     cut = lambda k: [lax.slice_in_dim(t, k, k + 1, axis=dim) for t in terms]
-    came = [partner(total(cut(k)), sizes, dim, k) for k in range(1, sizes[dim])]
-    return cut(0) + after(came, *earlier)
+    return [total(cut(k)) for k in range(1, sizes[dim])], cut(0)
+
+
+def fold(sent, stays, sizes, dim):
+    return stays + [partner(part, sizes, dim, k + 1) for k, part in enumerate(sent)]
 
 
 def both_halves(rows, sizes):
@@ -371,16 +374,20 @@
         rows = lax.dynamic_slice_in_dim(rows, my_dp * share, share, 0)
         return [rows[:, i * half : (i + 1) * half].reshape(1, 1, 1, 1, share, half) for i in range(2)]
 
-    x1 = [spread(p, sizes, 2) for p in mine(tokens)]
-    x2 = [spread(p, sizes, turn[0]) for p, turn in zip(x1, turns)]
+    halves = lambda rows: [rows[..., i * half : (i + 1) * half] for i in range(2)]
+    mine = lambda rows: lax.dynamic_slice_in_dim(rows, my_dp * share, share, 0)[None, None, None, None]
+    x0 = mine(tokens)
+    x1 = spread(x0, sizes, 2)
+    x2 = [spread(p, sizes, turn[0]) for p, turn in zip(halves(x1), turns)]
+    c1 = spread(after(mine(cotangent), x1), sizes, 2, x2)
     x3 = [spread(p, sizes, turn[1]) for p, turn in zip(x2, turns)]
     own_x = flat(x3)
     other_x = [partner(p, sizes, 0, 1) for p in own_x]
-    c1 = [spread(p, sizes, 2) for p in after(mine(cotangent), x1)]
-
-    info = jnp.concatenate([expert_ids.astype(F32), gates], axis=1).T
+
+    info = jnp.concatenate([after(expert_ids, x0).astype(F32), gates], axis=1).T
     info = info.reshape(2 * top, dp, share)[:, shares_at].reshape(1, 1, 1, 1, 2 * top, tok)
-    info = spread(spread(after(info, x1), sizes, 2), sizes, 1).reshape(experts // 2, 2 * top, tok)
+    info = spread(info, sizes, 2, x1)
+    info = spread(info, sizes, 1, x2).reshape(experts // 2, 2 * top, tok)
     info = jnp.stack([info, partner(info, sizes, 0, 1)])
 
     hit = info[:, :, :top] == me.astype(F32)
@@ -394,47 +401,45 @@
     gate = gate.reshape(2, -1, 1, GROUP * tok)
 
     pad = -units % 128
+    first = after(me * units, x1)
     widen = lambda m: jnp.pad(m, ((0, pad), (0, 0)))
-    columns = lambda m: widen(lax.dynamic_slice_in_dim(m, me * units, units, 1).T)
+    columns = lambda m: widen(lax.dynamic_slice_in_dim(m, first, units, 1).T)
     sgu = jnp.concatenate([columns(s_gate), columns(s_up)], axis=0)
-    sd = widen(lax.dynamic_slice_in_dim(s_down, me * units, units, 0))
+    sd = widen(lax.dynamic_slice_in_dim(s_down, first, units, 0))
     weights = (w_gate.swapaxes(1, 2), w_up.swapaxes(1, 2), w_down, sgu, sd)
 
     rows = experts // 2 * slots
-    ahead0 = forward_half(place[0], gate[0], own_x, weights, rows)
-    c2 = [spread(p, sizes, turn[0], ahead0[0]) for p, turn in zip(after(c1, x3), turns)]
-    ahead1 = forward_half(place[1], gate[1], other_x, weights, rows)
+    c2 = [spread(p, sizes, turn[0]) for p, turn in zip(halves(after(c1, x3)), turns)]
+    ahead0 = forward_half(after(place[0], c2), gate[0], own_x, weights, rows)
+    ahead1 = forward_half(place[1], gate[1], after(other_x, ahead0[0]), weights, rows)
     c3 = [spread(p, sizes, turn[1], ahead1[0]) for p, turn in zip(c2, turns)]
     own_c = flat(c3)
     back0 = backward_half(place[0], gate[0], own_c, weights, ahead0, rows)
-    other_c, out_came = after(
-        ([partner(p, sizes, 0, 1) for p in own_c], [partner(p, sizes, 0, 1) for p in full(ahead1[:2])]),
-        back0[0],
-    )
-    back1 = backward_half(place[1], gate[1], other_c, weights, ahead1, rows)
-
+    out_came = after([partner(p, sizes, 0, 1) for p in full(ahead1[:2])], back0[0])
     out = [list(t) for t in zip(full(ahead0[:2]), out_came)]
-    out = [fold(t, sizes, turn[1], back1[0]) for t, turn in zip(out, turns)]
+    out = [parts_for(t, sizes, turn[1]) for t, turn in zip(out, turns)]
+    other_c = after([partner(p, sizes, 0, 1) for p in own_c], back0[0])
+    back1 = backward_half(
+        after(place[1], [sent for sent, _ in out]), gate[1], other_c, weights, ahead1, rows
+    )
+
+    out = [fold(*t, sizes, turn[1]) for t, turn in zip(out, turns)]
+    out = [parts_for(after(t, back1[0]), sizes, turn[0]) for t, turn in zip(out, turns)]
+    out_sent = [sent for sent, _ in out]
     ga, gb, da, db = shared_grads(
-        [back0[5], back1[5]],
+        after([back0[5], back1[5]], [sent for sent, _ in out]),
         [ahead0[7], ahead1[7]],
         [own_x[0], other_x[0], own_x[1], other_x[1]],
         [own_c[0], other_c[0], own_c[1], other_c[1]],
     )
-    out = [fold(t, sizes, turn[0], ga) for t, turn in zip(out, turns)]
-    dx_came = after([partner(p, sizes, 0, 1) for p in full(back1[:2])], ga)
+    dx_came = after([partner(p, sizes, 0, 1) for p in full(after(back1[:2], out_sent))], ga)
     dx = [list(t) for t in zip(full(back0[:2]), dx_came)]
-    grad_wg, grad_wu, grad_wd = expert_grads(
-        [ahead0[2], ahead1[2]], [back0[2], back1[2]], [back0[3], back1[3]], [back0[4], back1[4]],
-        [ahead0[5], ahead1[5]],
-    )
-    dx = [fold(t, sizes, turn[1], grad_wg) for t, turn in zip(dx, turns)]
-    out = [fold(t, sizes, 2, grad_wg) for t in out]
-    moe_out = both_halves(jnp.concatenate([total(t).reshape(share, half) for t in out], axis=1), sizes)
-    dx = [fold(t, sizes, turn[0]) for t, turn in zip(dx, turns)]
-    dx = [fold(t, sizes, 2) for t in dx]
-    token_grads = both_halves(jnp.concatenate([total(t).reshape(share, half) for t in dx], axis=1), sizes)
-
+    dx = [parts_for(t, sizes, turn[1]) for t, turn in zip(dx, turns)]
+    out = [fold(*t, sizes, turn[0]) for t, turn in zip(out, turns)]
+    out = after(out, [sent for sent, _ in dx])
+    out = [jnp.concatenate(p, axis=5) for p in zip(*out)]
+    out = parts_for(out, sizes, 2)
+    ga, gb, da, db = after((ga, gb, da, db), out[0])
     unit = units + pad
     both = jnp.concatenate([ga, gb], axis=1)
     grads = jnp.concatenate(
@@ -442,7 +447,7 @@
     ).reshape(3 * units, experts, width // experts)
     index = np.arange(experts).reshape(sizes[2], sizes[1], 2).transpose(2, 1, 0).reshape(-1)
     where = jnp.asarray(np.argsort(index), jnp.int32)[me ^ jnp.arange(experts, dtype=jnp.int32)]
-    score = jnp.stack([back0[6], back1[6]]).reshape(experts, dp, share)
+    score = jnp.stack(after([back0[6], back1[6]], ga)).reshape(experts, dp, share)
     score = score[where][:, shares_at].reshape(experts, tok)
     block = grads.shape[2]
     lines = -(-tok // block)
@@ -463,6 +468,23 @@
     for k in range(1, dp):
         gate_grads = gate_grads + partner(gate_part, sizes, 3, k)
 
+    grad_wg, grad_wu, grad_wd = expert_grads(
+        [ahead0[2], ahead1[2]],
+        after([back0[2], back1[2]], send),
+        [back0[3], back1[3]],
+        [back0[4], back1[4]],
+        [ahead0[5], ahead1[5]],
+    )
+    out, dx = after(
+        (fold(*out, sizes, 2), [fold(*t, sizes, turn[1]) for t, turn in zip(dx, turns)]), grad_wg
+    )
+    dx = [parts_for(t, sizes, turn[0]) for t, turn in zip(dx, turns)]
+    out = after(out, [sent for sent, _ in dx])
+    moe_out = both_halves(total(out).reshape(share, width), sizes)
+    dx = [fold(*t, sizes, turn[0]) for t, turn in zip(dx, turns)]
+    dx = [jnp.concatenate(p, axis=5) for p in zip(*dx)]
+    dx = fold(*parts_for(dx, sizes, 2), sizes, 2)
+    token_grads = both_halves(total(dx).reshape(share, width), sizes)
     grad_wg, grad_wu = grad_wg.swapaxes(1, 2), grad_wu.swapaxes(1, 2)
     return (moe_out, token_grads, gate_grads, grad_wg, grad_wu, grad_wd, grad_sg, grad_su, grad_sd)
 

time: 334 us -> 322 us (0.964)
  local copies, waits for them, and re-layouts: 22 us -> 44.5 us
  waiting for transfers between devices: 96.6 us -> 76.7 us
  starting transfers between devices: 71.6 us -> 52.1 us
    ppermute x56 -> x44, starting transfers between devices: 65.5 us -> 45.4 us  [partner(): lax.ppermute(array, axis, [(i, i ^ mask) for i in range(lax.axis_size(axi...]
    ppermute x56 -> x44, waiting for transfers between devices: 96.6 us -> 76.7 us  [partner(): lax.ppermute(array, axis, [(i, i ^ mask) for i in range(lax.axis_size(axi...]
    slice x2 -> x33, local copies, waits for them, and re-layouts: 1.25 us -> 18.4 us  [the longest x29 17 us: parts_for(): cut = lambda k: [lax.slice_in_dim(t, k, k + 1, axis=dim) for t in terms]]
    concatenate x11, other arithmetic: 3.61 us -> 10.3 us  [spread(): return jnp.concatenate([out] + after(came, *earlier), axis=dim)]
    reshape x4 -> x0, other arithmetic: 4.96 us -> none  [local(): total(t).reshape(share, half)]
    unnamed x42 -> x87, local copies, waits for them, and re-layouts: 5.72 us -> 9.11 us
    convert_element_type x12 -> x13, other arithmetic: 23.5 us -> 22.8 us  [total(): return out.astype(BF16)]
  transfers between devices with their start and end apart: 57 -> 45, of which waited for: 28 -> 12; matrix products, arithmetic and copies ran while one was open for 15% -> 20% of each run, Pallas kernels for 24% -> 32%
where the time goes in v1:
time: 322 us; the launch traced here: 316 us
  Pallas kernels  99.9 us (31%)
  waiting for transfers between devices  76.7 us (24%)
  starting transfers between devices  52.1 us (16%)
  local copies, waits for them, and re-layouts  44.5 us (14%)
  other arithmetic  40.9 us (13%)
    ppermute x44, waiting for transfers between devices, partner(): lax.ppermute(array, axis, [(i, i ^ mask) for i in range(lax.axis_size(axi...  76.7 us
    pallas_call x4, Pallas kernels, half_call(): pl.pallas_call(kernel, grid=(groups,), in_specs=[spec_info(tokens)] * 2 +...  73.8 us
    ppermute x44, starting transfers between devices, partner(): lax.ppermute(array, axis, [(i, i ^ mask) for i in range(lax.axis_size(axi...  45.4 us
    convert_element_type x13, other arithmetic, total(): return out.astype(BF16)  22.8 us
    slice x29, local copies, waits for them, and re-layouts, parts_for(): cut = lambda k: [lax.slice_in_dim(t, k, k + 1, axis=dim) for t in terms]  17 us
    pallas_call x1, Pallas kernels, expert_grads(): pl.pallas_call(expert_grads_kernel, grid=(width // tile,), in_specs=[col]...  15.9 us
    concatenate x11, other arithmetic, spread(): return jnp.concatenate([out] + after(came, *earlier), axis=dim)  10.3 us
    pallas_call x1, Pallas kernels, shared_grads(): pl.pallas_call(shared_grads_kernel, grid=(half // tile,), in_specs=[spec_...  10.2 us
  transfers between devices with their start and end apart: 45, of which 12 were waited for; matrix products, arithmetic and copies ran while one was open for 20% of the time, Pallas kernels for 32%

profile of v1, /device:TPU:8, one launch (start us, length us, event | category | flops | bytes accessed | tf_op | source)
XLA Modules:
  0.0 316.2 jit_solution(12872586542363252490)
XLA Ops:
  6.9 2.8 collective-permute-start.5
  13.4 14.5 %collective-permute-done.5 = bf16[1,1,1,1,64,2048]{5,4,3,2,1,0:T(8,128)(2,1)S(1)} collective-permute-done((bf16[1,1,1,1,64,2048]{5,4,3,2,1,0:T(8,128)(2,1)S(1)}, bf16[1,1,1,1,64,2048]{5,4,3,2,1,0:T(8,128)(2,1)S(1)}, u32[]{:S(2)}, u32[]{:S(2)}) %collective-permute-start.5) | collective-permute-done | bytes 262176 | tf_op jit(solution)/shard_map/ppermute | solution.py:34
  27.9 3.6 %collective-permute-done.4 = bf16[1,1,1,1,64,2048]{5,4,3,2,1,0:T(8,128)(2,1)S(1)} collective-permute-done((bf16[1,1,1,1,64,2048]{5,4,3,2,1,0:T(8,128)(2,1)S(1)}, bf16[1,1,1,1,64,2048]{5,4,3,2,1,0:T(8,128)(2,1)S(1)}, u32[]{:S(2)}, u32[]{:S(2)}) %collective-permute-start.4) | collective-permute-done | bytes 262176 | tf_op jit(solution)/shard_map/ppermute | solution.py:34
  34.9 1.9 constant_dynamic-slice_fusion.1
  37.6 4.3 %collective-permute-start.11 = (bf16[1,1,1,1,64,2048]{5,4,3,2,1,0:T(8,128)(2,1)}, bf16[1,1,1,1,64,2048]{5,4,3,2,1,0:T(8,128)(2,1)}, u32[]{:S(2)}, u32[]{:S(2)}) collective-permute-start(bf16[1,1,1,1,64,2048]{5,4,3,2,1,0:T(8,128)(2,1)} %dynamic-slice_bitcast_fusion), channel_id=1, source_target_pairs={{0,8},{1,9},{2,10},{3,11},{4,12},{5,13},{6,14},{7,15},{8,0},{9,1},... | collective-permute-start | bytes 786440 | tf_op jit(solution)/shard_map/ppermute | solution.py:34
  49.1 8.6 %collective-permute-done.12 = bf16[1,1,1,1,64,2048]{5,4,3,2,1,0:T(8,128)(2,1)} collective-permute-done((bf16[1,1,1,1,64,2048]{5,4,3,2,1,0:T(8,128)(2,1)}, bf16[1,1,1,1,64,2048]{5,4,3,2,1,0:T(8,128)(2,1)}, u32[]{:S(2)}, u32[]{:S(2)}) %collective-permute-start.12) | collective-permute-done | bytes 262176 | tf_op jit(solution)/shard_map/ppermute | solution.py:34
  60.1 12.2 %collective-permute-done.6 = f32[1,1,4,1,12,128]{5,4,3,2,1,0:T(8,128)S(1)} collective-permute-done((f32[1,1,4,1,12,128]{5,4,3,2,1,0:T(8,128)S(1)}, f32[1,1,4,1,12,128]{5,4,3,2,1,0:T(8,128)S(1)}, u32[]{:S(2)}, u32[]{:S(2)}) %collective-permute-start.6) | collective-permute-done | bytes 24608 | tf_op jit(solution)/shard_map/ppermute | solution.py:34
  80.5 10.4 %collective-permute-done.15 = bf16[1,1,4,1,64,1024]{5,4,3,2,1,0:T(8,128)(2,1)} collective-permute-done((bf16[1,1,4,1,64,1024]{5,4,3,2,1,0:T(8,128)(2,1)S(1)}, bf16[1,1,4,1,64,1024]{5,4,3,2,1,0:T(8,128)(2,1)}, u32[]{:S(2)}, u32[]{:S(2)}) %collective-permute-start.15) | collective-permute-done | bytes 524320 | tf_op jit(solution)/shard_map/ppermute | solution.py:34
  90.9 2.1 pad_maximum_fusion.9
  96.2 17.4 %forward_half.2 = (bf16[1024,1024]{1,0:T(8,128)(2,1)}, bf16[1024,1024]{1,0:T(8,128)(2,1)}, bf16[512,2048]{1,0:T(8,128)(2,1)}, f32[512,704]{1,0:T(8,128)}, f32[51...) custom-call(s32[2,1,512]{2,1,0:T(1,128)} %bitcast.124, ...), custom_call_target="tpu_custom_call" | custom-call | flops 28454158336 | bytes 25632768 | tf_op jit(solution)/shard_map/forward_half/pallas_call | solution.py:217
  113.6 2.4 slice.395
  119.2 17.3 %forward_half.3 = (bf16[1024,1024]{1,0:T(8,128)(2,1)}, bf16[1024,1024]{1,0:T(8,128)(2,1)}, bf16[512,2048]{1,0:T(8,128)(2,1)}, f32[512,704]{1,0:T(8,128)}, f32[51...) custom-call(s32[2,1,512]{2,1,0:T(1,128)} %bitcast.120, ...), custom_call_target="tpu_custom_call" | custom-call | flops 28454158336 | bytes 25632768 | tf_op jit(solution)/shard_map/forward_half/pallas_call | solution.py:217
  138.0 2.3 pad_maximum_fusion.2
  141.7 19.5 %backward_half.2 = (bf16[1024,1024]{1,0:T(8,128)(2,1)}, bf16[1024,1024]{1,0:T(8,128)(2,1)}, bf16[512,2048]{1,0:T(8,128)(2,1)}, bf16[512,704]{1,0:T(8,128)(2,1)},...) custom-call(s32[2,1,512]{2,1,0:T(1,128)} %bitcast.125, f32[2,1,512]{2,1,0:T(1,128)} %bitcast.123, ...), custom_call_target="tpu_custom_call" | custom-call | flops 28454158336 | bytes 26619904 | tf_op jit(solution)/shard_map/backward_half/pallas_call | solution.py:217
  161.2 3.1 add_convert_fusion.3
  165.3 2.6 add_convert_fusion.2
  170.2 19.5 %backward_half.3 = (bf16[1024,1024]{1,0:T(8,128)(2,1)}, bf16[1024,1024]{1,0:T(8,128)(2,1)}, bf16[512,2048]{1,0:T(8,128)(2,1)}, bf16[512,704]{1,0:T(8,128)(2,1)},...) custom-call(s32[2,1,512]{2,1,0:T(1,128)} %bitcast.121, f32[2,1,512]{2,1,0:T(1,128)} %bitcast.119, ...), custom_call_target="tpu_custom_call" | custom-call | flops 28454158336 | bytes 26619904 | tf_op jit(solution)/shard_map/backward_half/pallas_call | solution.py:217
  194.0 2.6 add_convert_fusion.6
  200.6 10.2 %shared_grads.1 = (bf16[256,1024]{1,0:T(8,128)(2,1)}, bf16[256,1024]{1,0:T(8,128)(2,1)}, bf16[128,1024]{1,0:T(8,128)(2,1)}, bf16[128,1024]{1,0:T(8,128)(2,1)}) custom-call(bf16[1024,256]{1,0:T(8,128)(2,1)} %get-tuple-element.165.g0_ref, bf16[1024,256]{1,0:T(8,128)(2,1)} %get-tuple-element.166.g1_ref, bf16[1024,128]{1,0:T(8,128)(2,1)} %get-tuple-element.167.h0_ref, ...), custom_call_target="tpu_custom_call" | custom-call | flops 3221225472 | bytes 19922944 | tf_op jit(solution)/shard_map/shared_grads/pallas_call | solution.py:303
  210.8 2.4 slice.332
  213.2 2.7 add_convert_fusion.1
  216.0 2.7 add_convert_fusion
  225.4 3.3 %collective-permute-start.32 = (bf16[1,1,1,1,64,2048]{5,4,3,2,1,0:T(8,128)(2,1)}, bf16[1,1,1,1,64,2048]{5,4,3,2,1,0:T(8,128)(2,1)}, u32[]{:S(2)}, u32[]{:S(2)}) collective-permute-start(bf16[1,1,1,1,64,2048]{5,4,3,2,1,0:T(8,128)(2,1)} %get-tuple-element.261), channel_id=1, source_target_pairs={{0,8},{1,9},{2,10},{3,11},{4,12},{5,13},{6,14},{7,15},{8,0},{9,1},... | collective-permute-start | bytes 786440 | tf_op jit(solution)/shard_map/ppermute | solution.py:34
  236.7 6.6 %all-to-all-start = ((bf16[16,266,128]{2,1,0:T(8,128)(2,1)}), bf16[16,266,128]{2,1,0:T(8,128)(2,1)}, u32[]{:S(2)}, u32[]{:S(2)}) async-start(bf16[16,266,128]{2,1,0:T(8,128)(2,1)} %maximum_bitcast_fusion), calls=%async_computation | async-start | bytes 2228224 | tf_op jit(solution)/shard_map/all_to_all | solution.py:459
  243.3 15.9 %expert_grads.1 = (bf16[1,704,2048]{2,1,0:T(8,128)(2,1)}, bf16[1,704,2048]{2,1,0:T(8,128)(2,1)}, bf16[1,704,2048]{2,1,0:T(8,128)(2,1)}) custom-call(bf16[512,2048]{1,0:T(8,128)(2,1)} %get-tuple-element.181.x0_ref, bf16[512,2048]{1,0:T(8,128)(2,1)} %get-tuple-element.182.x1_ref, bf16[512,2048]{1,0:T(8,128)(2,1)} %get-tuple-element.196.c0_ref, ...), custom_call_target="tpu_custom_call" | custom-call | flops 17716740096 | bytes 21364736 | tf_op jit(solution)/shard_map/expert_grads/pallas_call | solution.py:344
  270.9 6.1 %collective-permute-done.37 = bf16[1,1,4,1,64,1024]{5,4,3,2,1,0:T(8,128)(2,1)S(1)} collective-permute-done((bf16[1,1,4,1,64,1024]{5,4,3,2,1,0:T(8,128)(2,1)S(1)}, bf16[1,1,4,1,64,1024]{5,4,3,2,1,0:T(8,128)(2,1)S(1)}, u32[]{:S(2)}, u32[]{:S(2)}) %collective-permute-start.37) | collective-permute-done | bytes 524320 | tf_op jit(solution)/shard_map/ppermute | solution.py:34
  277.0 3.1 collective-permute-done.38
  285.9 2.4 gather_fusion.4
  288.3 6.7 %collective-permute-done.40 = bf16[1,1,1,1,64,2048]{5,4,3,2,1,0:T(8,128)(2,1)} collective-permute-done((bf16[1,1,1,1,64,2048]{5,4,3,2,1,0:T(8,128)(2,1)S(1)}, bf16[1,1,1,1,64,2048]{5,4,3,2,1,0:T(8,128)(2,1)}, u32[]{:S(2)}, u32[]{:S(2)}) %collective-permute-start.40) | collective-permute-done | bytes 262176 | tf_op jit(solution)/shard_map/ppermute | solution.py:34
  296.3 7.6 %collective-permute-done.41 = bf16[1,1,1,1,64,2048]{5,4,3,2,1,0:T(8,128)(2,1)} collective-permute-done((bf16[1,1,1,1,64,2048]{5,4,3,2,1,0:T(8,128)(2,1)}, bf16[1,1,1,1,64,2048]{5,4,3,2,1,0:T(8,128)(2,1)}, u32[]{:S(2)}, u32[]{:S(2)}) %collective-permute-start.41) | collective-permute-done | bytes 262176 | tf_op jit(solution)/shard_map/ppermute | solution.py:34
  305.4 1.8 collective-permute-start.42
  308.4 2.1 fusion.33
  (260 shorter events, 93.0 us)
Async XLA Ops:
  4.3 32.6 %collective-permute-start.2 = (f32[1,1,1,1,12,128]{5,4,3,2,1,0:T(8,128)S(1)}, f32[1,1,1,1,12,128]{5,4,3,2,1,0:T(8,128)S(1)}, u32[]{:S(2)}, u32[]{:S(2)}) collective-permute-start(f32[1,1,1,1,12,128]{5,4,3,2,1,0:T(8,128)S(1)} %reshape.197), channel_id=1, source_target_pairs={{0,12},{1,13},{2,14},{3,15},{4,8},{5,9},{6,10},{7,11},{8,4},{9,5},... | collective-permute-start | bytes 18440 | tf_op jit(solution)/shard_map/ppermute | solution.py:34
  5.8 31.7 %collective-permute-start.1 = (f32[1,1,1,1,12,128]{5,4,3,2,1,0:T(8,128)S(1)}, f32[1,1,1,1,12,128]{5,4,3,2,1,0:T(8,128)S(1)}, u32[]{:S(2)}, u32[]{:S(2)}) collective-permute-start(f32[1,1,1,1,12,128]{5,4,3,2,1,0:T(8,128)S(1)} %reshape.197), channel_id=1, source_target_pairs={{0,8},{1,9},{2,10},{3,11},{4,12},{5,13},{6,14},{7,15},{8,0},{9,1},... | collective-permute-start | bytes 18440 | tf_op jit(solution)/shard_map/ppermute | solution.py:34
  6.9 21.0 %collective-permute-start.5 = (bf16[1,1,1,1,64,2048]{5,4,3,2,1,0:T(8,128)(2,1)S(1)}, bf16[1,1,1,1,64,2048]{5,4,3,2,1,0:T(8,128)(2,1)S(1)}, u32[]{:S(2)}, u32[]{:S(2)}) collective-permute-start(bf16[1,1,1,1,64,2048]{5,4,3,2,1,0:T(8,128)(2,1)S(1)} %dynamic-slice_bitcast_fusion.1), channel_id=1, source_target_pairs={{0,12},{1,13},{2,14},{3,15},{4,8},{5,9},{6,10},{7,11},{8,4},{9,5},... | collective-permute-start | bytes 786440 | tf_op jit(solution)/shard_map/ppermute | solution.py:34
  9.8 21.8 %collective-permute-start.4 = (bf16[1,1,1,1,64,2048]{5,4,3,2,1,0:T(8,128)(2,1)S(1)}, bf16[1,1,1,1,64,2048]{5,4,3,2,1,0:T(8,128)(2,1)S(1)}, u32[]{:S(2)}, u32[]{:S(2)}) collective-permute-start(bf16[1,1,1,1,64,2048]{5,4,3,2,1,0:T(8,128)(2,1)S(1)} %dynamic-slice_bitcast_fusion.1), channel_id=1, source_target_pairs={{0,8},{1,9},{2,10},{3,11},{4,12},{5,13},{6,14},{7,15},{8,0},{9,1},... | collective-permute-start | bytes 786440 | tf_op jit(solution)/shard_map/ppermute | solution.py:34
  10.7 20.9 %collective-permute-start.3 = (bf16[1,1,1,1,64,2048]{5,4,3,2,1,0:T(8,128)(2,1)S(1)}, bf16[1,1,1,1,64,2048]{5,4,3,2,1,0:T(8,128)(2,1)S(1)}, u32[]{:S(2)}, u32[]{:S(2)}) collective-permute-start(bf16[1,1,1,1,64,2048]{5,4,3,2,1,0:T(8,128)(2,1)S(1)} %dynamic-slice_bitcast_fusion.1), channel_id=1, source_target_pairs={{0,4},{1,5},{2,6},{3,7},{4,0},{5,1},{6,2},{7,3},{8,12},{9,13},{10,... | collective-permute-start | bytes 786440 | tf_op jit(solution)/shard_map/ppermute | solution.py:34
  36.8 20.9 %collective-permute-start.12 = (bf16[1,1,1,1,64,2048]{5,4,3,2,1,0:T(8,128)(2,1)}, bf16[1,1,1,1,64,2048]{5,4,3,2,1,0:T(8,128)(2,1)}, u32[]{:S(2)}, u32[]{:S(2)}) collective-permute-start(bf16[1,1,1,1,64,2048]{5,4,3,2,1,0:T(8,128)(2,1)} %dynamic-slice_bitcast_fusion), channel_id=1, source_target_pairs={{0,12},{1,13},{2,14},{3,15},{4,8},{5,9},{6,10},{7,11},{8,4},{9,5},... | collective-permute-start | bytes 786440 | tf_op jit(solution)/shard_map/ppermute | solution.py:34
  37.6 22.6 %collective-permute-start.11 = (bf16[1,1,1,1,64,2048]{5,4,3,2,1,0:T(8,128)(2,1)}, bf16[1,1,1,1,64,2048]{5,4,3,2,1,0:T(8,128)(2,1)}, u32[]{:S(2)}, u32[]{:S(2)}) collective-permute-start(bf16[1,1,1,1,64,2048]{5,4,3,2,1,0:T(8,128)(2,1)} %dynamic-slice_bitcast_fusion), channel_id=1, source_target_pairs={{0,8},{1,9},{2,10},{3,11},{4,12},{5,13},{6,14},{7,15},{8,0},{9,1},... | collective-permute-start | bytes 786440 | tf_op jit(solution)/shard_map/ppermute | solution.py:34
  41.9 18.2 %collective-permute-start.10 = (bf16[1,1,1,1,64,2048]{5,4,3,2,1,0:T(8,128)(2,1)}, bf16[1,1,1,1,64,2048]{5,4,3,2,1,0:T(8,128)(2,1)}, u32[]{:S(2)}, u32[]{:S(2)}) collective-permute-start(bf16[1,1,1,1,64,2048]{5,4,3,2,1,0:T(8,128)(2,1)} %dynamic-slice_bitcast_fusion), channel_id=1, source_target_pairs={{0,4},{1,5},{2,6},{3,7},{4,0},{5,1},{6,2},{7,3},{8,12},{9,13},{10,... | collective-permute-start | bytes 786440 | tf_op jit(solution)/shard_map/ppermute | solution.py:34
  45.8 28.0 %collective-permute-start.14 = (bf16[1,2,4,1,64,1024]{5,4,3,2,1,0:T(8,128)(2,1)S(1)}, bf16[1,2,4,1,64,1024]{5,4,3,2,1,0:T(8,128)(2,1)S(1)}, u32[]{:S(2)}, u32[]{:S(2)}) collective-permute-start(bf16[1,2,4,1,64,1024]{5,4,3,2,1,0:T(8,128)(2,1)S(1)} %pad_maximum_fusion.7), channel_id=1, source_target_pairs={{0,16},{16,0},{1,17},{17,1},{2,18},{18,2},{3,19},{19,3},{4,20},{20... | collective-permute-start | bytes 3145736 | tf_op jit(solution)/shard_map/ppermute | solution.py:34
  47.5 26.6 %collective-permute-start.13 = (bf16[1,1,4,2,64,1024]{5,4,3,2,1,0:T(8,128)(2,1)S(1)}, bf16[1,1,4,2,64,1024]{5,4,3,2,1,0:T(8,128)(2,1)S(1)}, u32[]{:S(2)}, u32[]{:S(2)}) collective-permute-start(bf16[1,1,4,2,64,1024]{5,4,3,2,1,0:T(8,128)(2,1)S(1)} %pad_maximum_fusion.6), channel_id=1, source_target_pairs={{0,2},{1,3},{2,0},{3,1},{4,6},{5,7},{6,4},{7,5},{8,10},{9,11},{10,... | collective-permute-start | bytes 3145736 | tf_op jit(solution)/shard_map/ppermute | solution.py:34
  78.1 14.9 %collective-permute-start.16 = (bf16[1,1,4,1,64,1024]{5,4,3,2,1,0:T(8,128)(2,1)S(1)}, bf16[1,1,4,1,64,1024]{5,4,3,2,1,0:T(8,128)(2,1)S(1)}, u32[]{:S(2)}, u32[]{:S(2)}) collective-permute-start(bf16[1,1,4,1,64,1024]{5,4,3,2,1,0:T(8,128)(2,1)S(1)} %get-tuple-element.268), channel_id=1, source_target_pairs={{0,2},{1,3},{2,0},{3,1},{4,6},{5,7},{6,4},{7,5},{8,10},{9,11},{10,... | collective-permute-start | bytes 1572872 | tf_op jit(solution)/shard_map/ppermute | solution.py:34
  80.0 37.2 %collective-permute-start.17 = (bf16[1024,1024]{1,0:T(8,128)(2,1)}, bf16[1024,1024]{1,0:T(8,128)(2,1)S(1)}, u32[]{:S(2)}, u32[]{:S(2)}) collective-permute-start(bf16[1024,1024]{1,0:T(8,128)(2,1)} %bitcast.80), channel_id=1, source_target_pairs={{0,1},{1,0},{2,3},{3,2},{4,5},{5,4},{6,7},{7,6},{8,9},{9,8},{10,11... | collective-permute-start | bytes 6291464 | tf_op jit(solution)/shard_map/ppermute | solution.py:34
  80.0 37.2 %collective-permute-start.18 = (bf16[1024,1024]{1,0:T(8,128)(2,1)S(1)}, bf16[1024,1024]{1,0:T(8,128)(2,1)S(1)}, u32[]{:S(2)}, u32[]{:S(2)}) collective-permute-start(bf16[1024,1024]{1,0:T(8,128)(2,1)S(1)} %bitcast.77), channel_id=1, source_target_pairs={{0,1},{1,0},{2,3},{3,2},{4,5},{5,4},{6,7},{7,6},{8,9},{9,8},{10,11... | collective-permute-start | bytes 6291464 | tf_op jit(solution)/shard_map/ppermute | solution.py:34
  94.1 42.5 %collective-permute-start.22 = (bf16[1,2,4,1,64,1024]{5,4,3,2,1,0:T(8,128)(2,1)}, bf16[1,2,4,1,64,1024]{5,4,3,2,1,0:T(8,128)(2,1)}, u32[]{:S(2)}, u32[]{:S(2)}) collective-permute-start(bf16[1,2,4,1,64,1024]{5,4,3,2,1,0:T(8,128)(2,1)} %pad_maximum_fusion.10), channel_id=1, source_target_pairs={{0,16},{16,0},{1,17},{17,1},{2,18},{18,2},{3,19},{19,3},{4,20},{20... | collective-permute-start | bytes 3145736 | tf_op jit(solution)/shard_map/ppermute | solution.py:34
  95.1 42.9 %collective-permute-start.21 = (bf16[1,1,4,2,64,1024]{5,4,3,2,1,0:T(8,128)(2,1)}, bf16[1,1,4,2,64,1024]{5,4,3,2,1,0:T(8,128)(2,1)}, u32[]{:S(2)}, u32[]{:S(2)}) collective-permute-start(bf16[1,1,4,2,64,1024]{5,4,3,2,1,0:T(8,128)(2,1)} %pad_maximum_fusion.9), channel_id=1, source_target_pairs={{0,2},{1,3},{2,0},{3,1},{4,6},{5,7},{6,4},{7,5},{8,10},{9,11},{10,... | collective-permute-start | bytes 3145736 | tf_op jit(solution)/shard_map/ppermute | solution.py:34
  140.4 28.5 %collective-permute-start.24 = (bf16[1024,1024]{1,0:T(8,128)(2,1)S(1)}, bf16[1024,1024]{1,0:T(8,128)(2,1)S(1)}, u32[]{:S(2)}, u32[]{:S(2)}) collective-permute-start(bf16[1024,1024]{1,0:T(8,128)(2,1)S(1)} %bitcast.86), channel_id=1, source_target_pairs={{0,1},{1,0},{2,3},{3,2},{4,5},{5,4},{6,7},{7,6},{8,9},{9,8},{10,11... | collective-permute-start | bytes 6291464 | tf_op jit(solution)/shard_map/ppermute | solution.py:34
  140.4 28.5 %collective-permute-start.25 = (bf16[1024,1024]{1,0:T(8,128)(2,1)S(1)}, bf16[1024,1024]{1,0:T(8,128)(2,1)}, u32[]{:S(2)}, u32[]{:S(2)}) collective-permute-start(bf16[1024,1024]{1,0:T(8,128)(2,1)S(1)} %bitcast.83), channel_id=1, source_target_pairs={{0,1},{1,0},{2,3},{3,2},{4,5},{5,4},{6,7},{7,6},{8,9},{9,8},{10,11... | collective-permute-start | bytes 6291464 | tf_op jit(solution)/shard_map/ppermute | solution.py:34
  140.9 20.2 %collective-permute-start.20 = (bf16[1,2,4,2,64,1024]{5,4,3,2,1,0:T(8,128)(2,1)}, bf16[1,2,4,2,64,1024]{5,4,3,2,1,0:T(8,128)(2,1)}, u32[]{:S(2)}, u32[]{:S(2)}) collective-permute-start(bf16[1,2,4,2,64,1024]{5,4,3,2,1,0:T(8,128)(2,1)} %bitcast.22), channel_id=1, source_target_pairs={{0,1},{1,0},{2,3},{3,2},{4,5},{5,4},{6,7},{7,6},{8,9},{9,8},{10,11... | collective-permute-start | bytes 6291464 | tf_op jit(solution)/shard_map/ppermute | solution.py:34
  141.0 20.1 %collective-permute-start.19 = (bf16[1,2,4,2,64,1024]{5,4,3,2,1,0:T(8,128)(2,1)}, bf16[1,2,4,2,64,1024]{5,4,3,2,1,0:T(8,128)(2,1)}, u32[]{:S(2)}, u32[]{:S(2)}) collective-permute-start(bf16[1,2,4,2,64,1024]{5,4,3,2,1,0:T(8,128)(2,1)} %bitcast.21), channel_id=1, source_target_pairs={{0,1},{1,0},{2,3},{3,2},{4,5},{5,4},{6,7},{7,6},{8,9},{9,8},{10,11... | collective-permute-start | bytes 6291464 | tf_op jit(solution)/shard_map/ppermute | solution.py:34
  164.3 28.7 %collective-permute-start.23 = (bf16[1,1,4,2,64,1024]{5,4,3,2,1,0:T(8,128)(2,1)}, bf16[1,1,4,2,64,1024]{5,4,3,2,1,0:T(8,128)(2,1)S(1)}, u32[]{:S(2)}, u32[]{:S(2)}) collective-permute-start(bf16[1,1,4,2,64,1024]{5,4,3,2,1,0:T(8,128)(2,1)} %add_convert_fusion.3), channel_id=1, source_target_pairs={{0,2},{1,3},{2,0},{3,1},{4,6},{5,7},{6,4},{7,5},{8,10},{9,11},{10,... | collective-permute-start | bytes 3145736 | tf_op jit(solution)/shard_map/ppermute | solution.py:34
  167.9 25.0 %collective-permute-start.27 = (bf16[1,2,4,1,64,1024]{5,4,3,2,1,0:T(8,128)(2,1)}, bf16[1,2,4,1,64,1024]{5,4,3,2,1,0:T(8,128)(2,1)}, u32[]{:S(2)}, u32[]{:S(2)}) collective-permute-start(bf16[1,2,4,1,64,1024]{5,4,3,2,1,0:T(8,128)(2,1)} %add_convert_fusion.2), channel_id=1, source_target_pairs={{0,16},{16,0},{1,17},{17,1},{2,18},{18,2},{3,19},{19,3},{4,20},{20... | collective-permute-start | bytes 3145736 | tf_op jit(solution)/shard_map/ppermute | solution.py:34
  198.4 20.3 %collective-permute-start.28 = (bf16[1,1,4,1,64,1024]{5,4,3,2,1,0:T(8,128)(2,1)}, bf16[1,1,4,1,64,1024]{5,4,3,2,1,0:T(8,128)(2,1)S(1)}, u32[]{:S(2)}, u32[]{:S(2)}) collective-permute-start(bf16[1,1,4,1,64,1024]{5,4,3,2,1,0:T(8,128)(2,1)} %add_convert_fusion.6), channel_id=1, source_target_pairs={{0,2},{1,3},{2,0},{3,1},{4,6},{5,7},{6,4},{7,5},{8,10},{9,11},{10,... | collective-permute-start | bytes 1572872 | tf_op jit(solution)/shard_map/ppermute | solution.py:34
  200.0 18.7 %collective-permute-start.26 = (bf16[1,1,4,1,64,1024]{5,4,3,2,1,0:T(8,128)(2,1)}, bf16[1,1,4,1,64,1024]{5,4,3,2,1,0:T(8,128)(2,1)S(1)}, u32[]{:S(2)}, u32[]{:S(2)}) collective-permute-start(bf16[1,1,4,1,64,1024]{5,4,3,2,1,0:T(8,128)(2,1)} %add_convert_fusion.7), channel_id=1, source_target_pairs={{0,16},{16,0},{1,17},{17,1},{2,18},{18,2},{3,19},{19,3},{4,20},{20... | collective-permute-start | bytes 1572872 | tf_op jit(solution)/shard_map/ppermute | solution.py:34
  223.4 37.3 %collective-permute-start.34 = (bf16[1,1,4,2,64,1024]{5,4,3,2,1,0:T(8,128)(2,1)}, bf16[1,1,4,2,64,1024]{5,4,3,2,1,0:T(8,128)(2,1)}, u32[]{:S(2)}, u32[]{:S(2)}) collective-permute-start(bf16[1,1,4,2,64,1024]{5,4,3,2,1,0:T(8,128)(2,1)} %add_convert_fusion.1), channel_id=1, source_target_pairs={{0,2},{1,3},{2,0},{3,1},{4,6},{5,7},{6,4},{7,5},{8,10},{9,11},{10,... | collective-permute-start | bytes 3145736 | tf_op jit(solution)/shard_map/ppermute | solution.py:34
  224.4 36.3 %collective-permute-start.35 = (bf16[1,2,4,1,64,1024]{5,4,3,2,1,0:T(8,128)(2,1)}, bf16[1,2,4,1,64,1024]{5,4,3,2,1,0:T(8,128)(2,1)}, u32[]{:S(2)}, u32[]{:S(2)}) collective-permute-start(bf16[1,2,4,1,64,1024]{5,4,3,2,1,0:T(8,128)(2,1)} %add_convert_fusion), channel_id=1, source_target_pairs={{0,16},{16,0},{1,17},{17,1},{2,18},{18,2},{3,19},{19,3},{4,20},{20... | collective-permute-start | bytes 3145736 | tf_op jit(solution)/shard_map/ppermute | solution.py:34
  225.4 35.3 %collective-permute-start.33 = (bf16[1,1,1,1,64,2048]{5,4,3,2,1,0:T(8,128)(2,1)}, bf16[1,1,1,1,64,2048]{5,4,3,2,1,0:T(8,128)(2,1)}, u32[]{:S(2)}, u32[]{:S(2)}) collective-permute-start(bf16[1,1,1,1,64,2048]{5,4,3,2,1,0:T(8,128)(2,1)} %get-tuple-element.260), channel_id=1, source_target_pairs={{0,12},{1,13},{2,14},{3,15},{4,8},{5,9},{6,10},{7,11},{8,4},{9,5},... | collective-permute-start | bytes 786440 | tf_op jit(solution)/shard_map/ppermute | solution.py:34
  225.4 35.3 %collective-permute-start.32 = (bf16[1,1,1,1,64,2048]{5,4,3,2,1,0:T(8,128)(2,1)}, bf16[1,1,1,1,64,2048]{5,4,3,2,1,0:T(8,128)(2,1)}, u32[]{:S(2)}, u32[]{:S(2)}) collective-permute-start(bf16[1,1,1,1,64,2048]{5,4,3,2,1,0:T(8,128)(2,1)} %get-tuple-element.261), channel_id=1, source_target_pairs={{0,8},{1,9},{2,10},{3,11},{4,12},{5,13},{6,14},{7,15},{8,0},{9,1},... | collective-permute-start | bytes 786440 | tf_op jit(solution)/shard_map/ppermute | solution.py:34
  228.7 32.0 %collective-permute-start.31 = (bf16[1,1,1,1,64,2048]{5,4,3,2,1,0:T(8,128)(2,1)}, bf16[1,1,1,1,64,2048]{5,4,3,2,1,0:T(8,128)(2,1)}, u32[]{:S(2)}, u32[]{:S(2)}) collective-permute-start(bf16[1,1,1,1,64,2048]{5,4,3,2,1,0:T(8,128)(2,1)} %get-tuple-element.262), channel_id=1, source_target_pairs={{0,4},{1,5},{2,6},{3,7},{4,0},{5,1},{6,2},{7,3},{8,12},{9,13},{10,... | collective-permute-start | bytes 786440 | tf_op jit(solution)/shard_map/ppermute | solution.py:34
  236.7 70.6 %all-to-all-start = ((bf16[16,266,128]{2,1,0:T(8,128)(2,1)}), bf16[16,266,128]{2,1,0:T(8,128)(2,1)}, u32[]{:S(2)}, u32[]{:S(2)}) async-start(bf16[16,266,128]{2,1,0:T(8,128)(2,1)} %maximum_bitcast_fusion), calls=%async_computation | async-start | bytes 2228224 | tf_op jit(solution)/shard_map/all_to_all | solution.py:459
  264.2 16.0 %collective-permute-start.38 = (bf16[1,1,4,1,64,1024]{5,4,3,2,1,0:T(8,128)(2,1)S(1)}, bf16[1,1,4,1,64,1024]{5,4,3,2,1,0:T(8,128)(2,1)S(1)}, u32[]{:S(2)}, u32[]{:S(2)}) collective-permute-start(bf16[1,1,4,1,64,1024]{5,4,3,2,1,0:T(8,128)(2,1)S(1)} %add_convert_fusion.4), channel_id=1, source_target_pairs={{0,2},{1,3},{2,0},{3,1},{4,6},{5,7},{6,4},{7,5},{8,10},{9,11},{10,... | collective-permute-start | bytes 1572872 | tf_op jit(solution)/shard_map/ppermute | solution.py:34
  269.4 15.6 %collective-permute-start.36 = (bf16[64,2048]{1,0:T(8,128)(2,1)S(1)}, bf16[64,2048]{1,0:T(8,128)(2,1)S(1)}, u32[]{:S(2)}, u32[]{:S(2)}) collective-permute-start(bf16[64,2048]{1,0:T(8,128)(2,1)S(1)} %bitcast.103), channel_id=1, source_target_pairs={{0,16},{16,0},{1,17},{17,1},{2,18},{18,2},{3,19},{19,3},{4,20},{20... | collective-permute-start | bytes 786440 | tf_op jit(solution)/shard_map/ppermute | solution.py:34
  284.5 19.5 %collective-permute-start.41 = (bf16[1,1,1,1,64,2048]{5,4,3,2,1,0:T(8,128)(2,1)}, bf16[1,1,1,1,64,2048]{5,4,3,2,1,0:T(8,128)(2,1)}, u32[]{:S(2)}, u32[]{:S(2)}) collective-permute-start(bf16[1,1,1,1,64,2048]{5,4,3,2,1,0:T(8,128)(2,1)} %get-tuple-element.259), channel_id=1, source_target_pairs={{0,12},{1,13},{2,14},{3,15},{4,8},{5,9},{6,10},{7,11},{8,4},{9,5},... | collective-permute-start | bytes 786440 | tf_op jit(solution)/shard_map/ppermute | solution.py:34
  (55 other events, 377.3 us)

commit v2 on v1

--- a/solution.py
+++ b/solution.py
@@ -11,6 +11,7 @@
 F32 = jnp.float32
 BF16 = jnp.bfloat16
 GROUP = 4
+FACTS = 128
 VMEM_LIMIT = 56 * 1024 * 1024
 
 
@@ -52,11 +53,14 @@
 
 def parts_for(terms, sizes, dim):
     cut = lambda k: [lax.slice_in_dim(t, k, k + 1, axis=dim) for t in terms]
-    return [total(cut(k)) for k in range(1, sizes[dim])], cut(0)
-
-
-def fold(sent, stays, sizes, dim):
-    return stays + [partner(part, sizes, dim, k + 1) for k, part in enumerate(sent)]
+    stays = cut(0)
+    if sizes[dim] > 2:
+        stays = lax.optimization_barrier(stays)
+    return [total(cut(k)) for k in range(1, sizes[dim])], stays
+
+
+def fold(sent, stays, sizes, dim, *earlier):
+    return stays + after([partner(part, sizes, dim, k + 1) for k, part in enumerate(sent)], *earlier)
 
 
 def both_halves(rows, sizes):
@@ -205,7 +209,7 @@
 
 def half_call(name, kernel, place, gate, parts, weights, more, outs, scratch):
     groups, _, tokens = place.shape
-    half = parts[0].shape[1]
+    half = parts[1].shape[1]
     ff = weights[0].shape[1]
     hbm = pl.BlockSpec(memory_space=pl.ANY)
     by_group = lambda n: spec_rows(n.shape[0] // groups, n.shape[1])
@@ -218,7 +222,7 @@
         kernel,
         grid=(groups,),
         in_specs=[spec_info(tokens)] * 2
-        + [by_group(p) for p in parts]
+        + [spec_rows(p.shape[0] // groups, half) for p in parts]
         + [hbm] * 3
         + [spec_whole(w) for w in weights[3:]]
         + [by_group(m) for m in more],
@@ -234,7 +238,7 @@
 
 
 def forward_half(place, gate, parts, weights, rows):
-    tokens, half = parts[0].shape
+    tokens, half = parts[1].shape
     ff, unit = weights[0].shape[1], weights[4].shape[0]
     shape = jax.ShapeDtypeStruct
     outs = [
@@ -251,7 +255,7 @@
 
 
 def backward_half(place, gate, parts, weights, ahead, rows):
-    tokens, half = parts[0].shape
+    tokens, half = parts[1].shape
     ff, unit = weights[0].shape[1], weights[4].shape[0]
     shape = jax.ShapeDtypeStruct
     outs = [
@@ -294,7 +298,7 @@
 
 
 def shared_grads(grads, hiddens, xs, cs):
-    rows, half = xs[0].shape
+    rows, half = xs[2].shape
     unit2, unit = grads[0].shape[1], hiddens[0].shape[1]
     tile = min(256, half)
     col = pl.BlockSpec((rows, tile), lambda i: (0, i))
@@ -367,7 +371,7 @@
     shares_at = my_dp ^ jnp.arange(dp, dtype=jnp.int32)
     turns = ((3, 1), (1, 3))
     shape = (1,) + sizes[1:] + (share, half)
-    flat = lambda parts: [p.reshape(-1, half) for p in parts]
+    flat = lambda parts: [p.reshape(-1, p.shape[5]) for p in parts]
     full = lambda parts: [p.reshape(shape) for p in parts]
 
     def mine(rows):
@@ -376,29 +380,31 @@
 
     halves = lambda rows: [rows[..., i * half : (i + 1) * half] for i in range(2)]
     mine = lambda rows: lax.dynamic_slice_in_dim(rows, my_dp * share, share, 0)[None, None, None, None]
-    x0 = mine(tokens)
+    high = lax.reduce_precision(gates, 8, 7)
+    facts = jnp.concatenate([expert_ids.astype(F32), high, gates - high], axis=1).astype(BF16)
+    facts = jnp.pad(facts, ((0, 0), (0, FACTS - facts.shape[1])))
+    x0 = mine(jnp.concatenate([tokens[:, :half], facts, tokens[:, half:]], axis=1))
     x1 = spread(x0, sizes, 2)
-    x2 = [spread(p, sizes, turn[0]) for p, turn in zip(halves(x1), turns)]
+    x1 = (x1[..., : half + FACTS], x1[..., half + FACTS :])
+    x2 = [spread(p, sizes, turn[0]) for p, turn in zip(x1, turns)]
     c1 = spread(after(mine(cotangent), x1), sizes, 2, x2)
     x3 = [spread(p, sizes, turn[1]) for p, turn in zip(x2, turns)]
     own_x = flat(x3)
     other_x = [partner(p, sizes, 0, 1) for p in own_x]
 
-    info = jnp.concatenate([after(expert_ids, x0).astype(F32), gates], axis=1).T
-    info = info.reshape(2 * top, dp, share)[:, shares_at].reshape(1, 1, 1, 1, 2 * top, tok)
-    info = spread(info, sizes, 2, x1)
-    info = spread(info, sizes, 1, x2).reshape(experts // 2, 2 * top, tok)
-    info = jnp.stack([info, partner(info, sizes, 0, 1)])
-
-    hit = info[:, :, :top] == me.astype(F32)
-    taken = jnp.any(hit, axis=2)
-    gate = jnp.sum(jnp.where(hit, info[:, :, top:], 0.0), axis=2)
     before = jnp.triu(jnp.ones((tok, tok), BF16), 1)
-    place = mm(taken.astype(BF16).reshape(experts, tok), before, 1, 0).astype(jnp.int32)
     start = slots * (jnp.arange(experts // 2, dtype=jnp.int32) % GROUP)
-    place = jnp.where(taken, place.reshape(taken.shape) + start[None, :, None], -1)
-    place = place.reshape(2, -1, 1, GROUP * tok)
-    gate = gate.reshape(2, -1, 1, GROUP * tok)
+
+    def routing(part):
+        known = part[:, half : half + 3 * top].astype(F32).T.reshape(3, top, experts // 2, tok)
+        hit = known[0] == me.astype(F32)
+        taken = jnp.any(hit, axis=0)
+        gate = jnp.sum(jnp.where(hit, known[1] + known[2], 0.0), axis=0)
+        place = mm(taken.astype(BF16), before, 1, 0).astype(jnp.int32) + start[:, None]
+        place = jnp.where(taken, place, -1)
+        return place.reshape(-1, 1, GROUP * tok), gate.reshape(-1, 1, GROUP * tok)
+
+    place, gate = zip(routing(own_x[0]), routing(other_x[0]))
 
     pad = -units % 128
     first = after(me * units, x1)
@@ -409,7 +415,7 @@
     weights = (w_gate.swapaxes(1, 2), w_up.swapaxes(1, 2), w_down, sgu, sd)
 
     rows = experts // 2 * slots
-    c2 = [spread(p, sizes, turn[0]) for p, turn in zip(halves(after(c1, x3)), turns)]
+    c2 = [spread(p, sizes, turn[0]) for p, turn in zip(after(halves(c1), x3), turns)]
     ahead0 = forward_half(after(place[0], c2), gate[0], own_x, weights, rows)
     ahead1 = forward_half(place[1], gate[1], after(other_x, ahead0[0]), weights, rows)
     c3 = [spread(p, sizes, turn[1], ahead1[0]) for p, turn in zip(c2, turns)]
@@ -423,11 +429,11 @@
         after(place[1], [sent for sent, _ in out]), gate[1], other_c, weights, ahead1, rows
     )
 
-    out = [fold(*t, sizes, turn[1]) for t, turn in zip(out, turns)]
-    out = [parts_for(after(t, back1[0]), sizes, turn[0]) for t, turn in zip(out, turns)]
+    out = [fold(*t, sizes, turn[1], back1[0]) for t, turn in zip(out, turns)]
+    out = [parts_for(t, sizes, turn[0]) for t, turn in zip(out, turns)]
     out_sent = [sent for sent, _ in out]
     ga, gb, da, db = shared_grads(
-        after([back0[5], back1[5]], [sent for sent, _ in out]),
+        after([back0[5], back1[5]], out_sent),
         [ahead0[7], ahead1[7]],
         [own_x[0], other_x[0], own_x[1], other_x[1]],
         [own_c[0], other_c[0], own_c[1], other_c[1]],
@@ -435,8 +441,8 @@
     dx_came = after([partner(p, sizes, 0, 1) for p in full(after(back1[:2], out_sent))], ga)
     dx = [list(t) for t in zip(full(back0[:2]), dx_came)]
     dx = [parts_for(t, sizes, turn[1]) for t, turn in zip(dx, turns)]
-    out = [fold(*t, sizes, turn[0]) for t, turn in zip(out, turns)]
-    out = after(out, [sent for sent, _ in dx])
+    dx_sent = [sent for sent, _ in dx]
+    out = [fold(*t, sizes, turn[0], dx_sent) for t, turn in zip(out, turns)]
     out = [jnp.concatenate(p, axis=5) for p in zip(*out)]
     out = parts_for(out, sizes, 2)
     ga, gb, da, db = after((ga, gb, da, db), out[0])
@@ -451,12 +457,17 @@
     score = score[where][:, shares_at].reshape(experts, tok)
     block = grads.shape[2]
     lines = -(-tok // block)
-    high = score.astype(BF16)
-    low = (score - high.astype(F32)).astype(BF16)
-    extra = jnp.pad(jnp.stack([high, low]), ((0, 0), (0, 0), (0, lines * block - tok)))
+    high = lax.reduce_precision(score, 8, 7)
+    extra = jnp.pad(jnp.stack([high, score - high]).astype(BF16), ((0, 0), (0, 0), (0, lines * block - tok)))
     extra = extra.reshape(2, experts, lines, block).transpose(0, 2, 1, 3)
     send = jnp.concatenate([grads, extra.reshape(2 * lines, experts, block)], axis=0).transpose(1, 0, 2)
+    dx = [fold(*t, sizes, turn[1], send) for t, turn in zip(dx, turns)]
+    dx = [parts_for(t, sizes, turn[0]) for t, turn in zip(dx, turns)]
+    dx_sent = [sent for sent, _ in dx]
     got = lax.all_to_all(send, "expert", split_axis=0, concat_axis=0, tiled=True)
+    got, out_came = after((got, fold(out[0], [], sizes, 2)), dx_sent)
+    out = out[1] + out_came
+    moe_out = both_halves(total(out).reshape(share, width), sizes)
     grad_sg = got[:, :units].reshape(experts * units, -1).T
     grad_su = got[:, units : 2 * units].reshape(experts * units, -1).T
     grad_sd = got[:, 2 * units : 3 * units].reshape(experts * units, -1)
@@ -468,23 +479,17 @@
     for k in range(1, dp):
         gate_grads = gate_grads + partner(gate_part, sizes, 3, k)
 
+    dx = [fold(*t, sizes, turn[0]) for t, turn in zip(dx, turns)]
+    dx = [jnp.concatenate(p, axis=5) for p in zip(*dx)]
+    dx = parts_for(dx, sizes, 2)
     grad_wg, grad_wu, grad_wd = expert_grads(
         [ahead0[2], ahead1[2]],
-        after([back0[2], back1[2]], send),
+        after([back0[2], back1[2]], dx[0]),
         [back0[3], back1[3]],
         [back0[4], back1[4]],
         [ahead0[5], ahead1[5]],
     )
-    out, dx = after(
-        (fold(*out, sizes, 2), [fold(*t, sizes, turn[1]) for t, turn in zip(dx, turns)]), grad_wg
-    )
-    dx = [parts_for(t, sizes, turn[0]) for t, turn in zip(dx, turns)]
-    out = after(out, [sent for sent, _ in dx])
-    moe_out = both_halves(total(out).reshape(share, width), sizes)
-    dx = [fold(*t, sizes, turn[0]) for t, turn in zip(dx, turns)]
-    dx = [jnp.concatenate(p, axis=5) for p in zip(*dx)]
-    dx = fold(*parts_for(dx, sizes, 2), sizes, 2)
-    token_grads = both_halves(total(dx).reshape(share, width), sizes)
+    token_grads = both_halves(total(fold(*dx, sizes, 2, grad_wg)).reshape(share, width), sizes)
     grad_wg, grad_wu = grad_wg.swapaxes(1, 2), grad_wu.swapaxes(1, 2)
     return (moe_out, token_grads, gate_grads, grad_wg, grad_wu, grad_wd, grad_sg, grad_su, grad_sd)
 

time: 322 us -> 328 us (1.019)
  waiting for transfers between devices: 76.7 us -> 90.9 us
  starting transfers between devices: 52.1 us -> 44.6 us
  other arithmetic: 40.9 us -> 48.2 us
  local copies, waits for them, and re-layouts: 44.5 us -> 37.3 us
    ppermute x44 -> x39, waiting for transfers between devices: 76.7 us -> 90.9 us  [partner(): lax.ppermute(array, axis, [(i, i ^ mask) for i in range(lax.axis_size(axi...]
    ppermute x44 -> x39, starting transfers between devices: 45.4 us -> 38.9 us  [partner(): lax.ppermute(array, axis, [(i, i ^ mask) for i in range(lax.axis_size(axi...]
    slice x29 -> x13, local copies, waits for them, and re-layouts: 17 us -> 13.6 us  [parts_for(): cut = lambda k: [lax.slice_in_dim(t, k, k + 1, axis=dim) for t in terms]]
    convert_element_type x13 -> x14, other arithmetic: 22.8 us -> 24.1 us  [total(): return out.astype(BF16)]
    unnamed x87 -> x54, local copies, waits for them, and re-layouts: 9.11 us -> 8.92 us
    concatenate x11 -> x9, other arithmetic: 10.3 us -> 10.4 us  [spread(): return jnp.concatenate([out] + after(came, *earlier), axis=dim)]
  transfers between devices with their start and end apart: 45 -> 40, of which waited for: 12 -> 14; matrix products, arithmetic and copies ran while one was open for 20% -> 23% of each run, Pallas kernels for 32% -> 31%
where the time goes in v2:
time: 328 us; the launch traced here: 323 us
  Pallas kernels  98.5 us (30%)
  waiting for transfers between devices  90.9 us (28%)
  other arithmetic  48.2 us (15%)
  starting transfers between devices  44.6 us (14%)
  local copies, waits for them, and re-layouts  37.3 us (11%)
    ppermute x39, waiting for transfers between devices, partner(): lax.ppermute(array, axis, [(i, i ^ mask) for i in range(lax.axis_size(axi...  90.9 us
    pallas_call x4, Pallas kernels, half_call(): pl.pallas_call(kernel, grid=(groups,), in_specs=[spec_info(tokens)] * 2 +...  72.8 us
    ppermute x39, starting transfers between devices, partner(): lax.ppermute(array, axis, [(i, i ^ mask) for i in range(lax.axis_size(axi...  38.9 us
    convert_element_type x14, other arithmetic, total(): return out.astype(BF16)  24.1 us
    pallas_call x1, Pallas kernels, expert_grads(): pl.pallas_call(expert_grads_kernel, grid=(width // tile,), in_specs=[col]...  16 us
    slice x13, local copies, waits for them, and re-layouts, parts_for(): cut = lambda k: [lax.slice_in_dim(t, k, k + 1, axis=dim) for t in terms]  13.6 us
    concatenate x9, other arithmetic, spread(): return jnp.concatenate([out] + after(came, *earlier), axis=dim)  10.4 us
    pallas_call x1, Pallas kernels, shared_grads(): pl.pallas_call(shared_grads_kernel, grid=(half // tile,), in_specs=[spec_...  9.71 us
  transfers between devices with their start and end apart: 40, of which 14 were waited for; matrix products, arithmetic and copies ran while one was open for 23% of the time, Pallas kernels for 31%

profile of v2, /device:TPU:8, one launch (start us, length us, event | category | flops | bytes accessed | tf_op | source)
XLA Modules:
  0.0 322.7 jit_solution(13488528595754570426)
XLA Ops:
  3.4 3.0 collective-permute-start.1
  6.9 7.9 %collective-permute-done = bf16[1,1,1,1,64,2176]{5,4,3,2,1,0:T(8,128)(2,1)S(1)} collective-permute-done((bf16[1,1,1,1,64,2176]{5,4,3,2,1,0:T(8,128)(2,1)S(1)}, bf16[1,1,1,1,64,2176]{5,4,3,2,1,0:T(8,128)(2,1)S(1)}, u32[]{:S(2)}, u32[]{:S(2)}) %collective-permute-start) | collective-permute-done | bytes 278560 | tf_op jit(solution)/shard_map/ppermute | solution.py:35
  14.8 10.7 %collective-permute-done.1 = bf16[1,1,1,1,64,2176]{5,4,3,2,1,0:T(8,128)(2,1)S(1)} collective-permute-done((bf16[1,1,1,1,64,2176]{5,4,3,2,1,0:T(8,128)(2,1)S(1)}, bf16[1,1,1,1,64,2176]{5,4,3,2,1,0:T(8,128)(2,1)S(1)}, u32[]{:S(2)}, u32[]{:S(2)}) %collective-permute-start.1) | collective-permute-done | bytes 278560 | tf_op jit(solution)/shard_map/ppermute | solution.py:35
  25.5 5.5 %collective-permute-done.2 = bf16[1,1,1,1,64,2176]{5,4,3,2,1,0:T(8,128)(2,1)S(1)} collective-permute-done((bf16[1,1,1,1,64,2176]{5,4,3,2,1,0:T(8,128)(2,1)S(1)}, bf16[1,1,1,1,64,2176]{5,4,3,2,1,0:T(8,128)(2,1)S(1)}, u32[]{:S(2)}, u32[]{:S(2)}) %collective-permute-start.2) | collective-permute-done | bytes 278560 | tf_op jit(solution)/shard_map/ppermute | solution.py:35
  32.8 3.0 collective-permute-start.6
  42.0 2.1 fusion.8.sgu_ref
  45.5 7.1 %collective-permute-done.3 = bf16[1,1,4,1,64,1152]{5,4,3,2,1,0:T(8,128)(2,1)S(1)} collective-permute-done((bf16[1,1,4,1,64,1152]{5,4,3,2,1,0:T(8,128)(2,1)S(1)}, bf16[1,1,4,1,64,1152]{5,4,3,2,1,0:T(8,128)(2,1)S(1)}, u32[]{:S(2)}, u32[]{:S(2)}) %collective-permute-start.3) | collective-permute-done | bytes 589856 | tf_op jit(solution)/shard_map/ppermute | solution.py:35
  54.2 3.5 %collective-permute-done.7 = bf16[1,1,1,1,64,2048]{5,4,3,2,1,0:T(8,128)(2,1)} collective-permute-done((bf16[1,1,1,1,64,2048]{5,4,3,2,1,0:T(8,128)(2,1)S(1)}, bf16[1,1,1,1,64,2048]{5,4,3,2,1,0:T(8,128)(2,1)}, u32[]{:S(2)}, u32[]{:S(2)}) %collective-permute-start.7) | collective-permute-done | bytes 262176 | tf_op jit(solution)/shard_map/ppermute | solution.py:35
  61.5 10.1 %collective-permute-done.9 = bf16[1,2,4,1,64,1024]{5,4,3,2,1,0:T(8,128)(2,1)S(1)} collective-permute-done((bf16[1,2,4,1,64,1024]{5,4,3,2,1,0:T(8,128)(2,1)S(1)}, bf16[1,2,4,1,64,1024]{5,4,3,2,1,0:T(8,128)(2,1)S(1)}, u32[]{:S(2)}, u32[]{:S(2)}) %collective-permute-start.9) | collective-permute-done | bytes 1048608 | tf_op jit(solution)/shard_map/ppermute | solution.py:35
  80.0 8.1 %collective-permute-done.11 = bf16[1,1,4,1,64,1024]{5,4,3,2,1,0:T(8,128)(2,1)S(1)} collective-permute-done((bf16[1,1,4,1,64,1024]{5,4,3,2,1,0:T(8,128)(2,1)}, bf16[1,1,4,1,64,1024]{5,4,3,2,1,0:T(8,128)(2,1)S(1)}, u32[]{:S(2)}, u32[]{:S(2)}) %collective-permute-start.11) | collective-permute-done | bytes 524320 | tf_op jit(solution)/shard_map/ppermute | solution.py:35
  88.0 2.1 pad_maximum_fusion.9
  90.2 2.2 pad_maximum_fusion.8
  94.6 16.9 %forward_half.2 = (bf16[1024,1024]{1,0:T(8,128)(2,1)}, bf16[1024,1024]{1,0:T(8,128)(2,1)}, bf16[512,2048]{1,0:T(8,128)(2,1)}, f32[512,704]{1,0:T(8,128)}, f32[51...) custom-call(s32[2,1,512]{2,1,0:T(1,128)} %bitcast.125, ...), custom_call_target="tpu_custom_call" | custom-call | flops 28454158336 | bytes 25894912 | tf_op jit(solution)/shard_map/forward_half/pallas_call | solution.py:221
  114.6 16.8 %forward_half.3 = (bf16[1024,1024]{1,0:T(8,128)(2,1)}, bf16[1024,1024]{1,0:T(8,128)(2,1)}, bf16[512,2048]{1,0:T(8,128)(2,1)}, f32[512,704]{1,0:T(8,128)}, f32[51...) custom-call(s32[2,1,512]{2,1,0:T(1,128)} %bitcast.127, ...), custom_call_target="tpu_custom_call" | custom-call | flops 28454158336 | bytes 25894912 | tf_op jit(solution)/shard_map/forward_half/pallas_call | solution.py:221
  132.9 2.3 pad_maximum_fusion.2
  136.6 19.5 %backward_half.2 = (bf16[1024,1024]{1,0:T(8,128)(2,1)}, bf16[1024,1024]{1,0:T(8,128)(2,1)}, bf16[512,2048]{1,0:T(8,128)(2,1)}, bf16[512,704]{1,0:T(8,128)(2,1)},...) custom-call(s32[2,1,512]{2,1,0:T(1,128)} %bitcast.126, f32[2,1,512]{2,1,0:T(1,128)} %bitcast.110, ...), custom_call_target="tpu_custom_call" | custom-call | flops 28454158336 | bytes 26619904 | tf_op jit(solution)/shard_map/backward_half/pallas_call | solution.py:221
  156.1 3.1 add_convert_fusion.2
  159.8 2.6 add_convert_fusion.3
  165.0 19.6 %backward_half.3 = (bf16[1024,1024]{1,0:T(8,128)(2,1)}, bf16[1024,1024]{1,0:T(8,128)(2,1)}, bf16[512,2048]{1,0:T(8,128)(2,1)}, bf16[512,704]{1,0:T(8,128)(2,1)},...) custom-call(s32[2,1,512]{2,1,0:T(1,128)} %bitcast.128, f32[2,1,512]{2,1,0:T(1,128)} %bitcast.112, ...), custom_call_target="tpu_custom_call" | custom-call | flops 28454158336 | bytes 26619904 | tf_op jit(solution)/shard_map/backward_half/pallas_call | solution.py:221
  184.7 2.3 add_convert_fusion.6
  187.3 2.4 add_convert_fusion.7
  202.9 9.7 %shared_grads.1 = (bf16[256,1024]{1,0:T(8,128)(2,1)}, bf16[256,1024]{1,0:T(8,128)(2,1)}, bf16[128,1024]{1,0:T(8,128)(2,1)}, bf16[128,1024]{1,0:T(8,128)(2,1)}) custom-call(bf16[1024,256]{1,0:T(8,128)(2,1)} %get-tuple-element.143.g0_ref, bf16[1024,256]{1,0:T(8,128)(2,1)} %get-tuple-element.144.g1_ref, bf16[1024,128]{1,0:T(8,128)(2,1)} %get-tuple-element.145.h0_ref, ...), custom_call_target="tpu_custom_call" | custom-call | flops 3221225472 | bytes 20447232 | tf_op jit(solution)/shard_map/shared_grads/pallas_call | solution.py:307
  212.6 3.1 add_convert_fusion
  221.7 2.5 collective-permute-start.27
  231.1 14.2 %collective-permute-done.30 = bf16[1,2,4,1,64,1024]{5,4,3,2,1,0:T(8,128)(2,1)} collective-permute-done((bf16[1,2,4,1,64,1024]{5,4,3,2,1,0:T(8,128)(2,1)}, bf16[1,2,4,1,64,1024]{5,4,3,2,1,0:T(8,128)(2,1)}, u32[]{:S(2)}, u32[]{:S(2)}) %collective-permute-start.30) | collective-permute-done | bytes 1048608 | tf_op jit(solution)/shard_map/ppermute | solution.py:35
  245.3 2.4 add_convert_fusion.4
  247.7 2.4 add_convert_fusion.5
  252.1 5.7 %all-to-all-start = ((bf16[16,266,128]{2,1,0:T(8,128)(2,1)}), bf16[16,266,128]{2,1,0:T(8,128)(2,1)}, u32[]{:S(2)}, u32[]{:S(2)}) async-start(bf16[16,266,128]{2,1,0:T(8,128)(2,1)} %maximum_bitcast_fusion), calls=%async_computation | async-start | bytes 2228224 | tf_op jit(solution)/shard_map/all_to_all | solution.py:467
  265.9 4.5 %collective-permute-start.35 = (bf16[1,1,1,1,64,2048]{5,4,3,2,1,0:T(8,128)(2,1)S(1)}, bf16[1,1,1,1,64,2048]{5,4,3,2,1,0:T(8,128)(2,1)S(1)}, u32[]{:S(2)}, u32[]{:S(2)}) collective-permute-start(bf16[1,1,1,1,64,2048]{5,4,3,2,1,0:T(8,128)(2,1)S(1)} %add_convert_fusion.10), channel_id=1, source_target_pairs={{0,8},{1,9},{2,10},{3,11},{4,12},{5,13},{6,14},{7,15},{8,0},{9,1},... | collective-permute-start | bytes 786440 | tf_op jit(solution)/shard_map/ppermute | solution.py:35
  271.6 16.0 %expert_grads.1 = (bf16[1,704,2048]{2,1,0:T(8,128)(2,1)}, bf16[1,704,2048]{2,1,0:T(8,128)(2,1)}, bf16[1,704,2048]{2,1,0:T(8,128)(2,1)}) custom-call(bf16[512,2048]{1,0:T(8,128)(2,1)} %get-tuple-element.180.x0_ref, bf16[512,2048]{1,0:T(8,128)(2,1)} %get-tuple-element.181.x1_ref, bf16[512,2048]{1,0:T(8,128)(2,1)} %get-tuple-element.184.c0_ref, ...), custom_call_target="tpu_custom_call" | custom-call | flops 17716740096 | bytes 21364736 | tf_op jit(solution)/shard_map/expert_grads/pallas_call | solution.py:348
  287.6 12.3 %collective-permute-done.35 = bf16[1,1,1,1,64,2048]{5,4,3,2,1,0:T(8,128)(2,1)S(1)} collective-permute-done((bf16[1,1,1,1,64,2048]{5,4,3,2,1,0:T(8,128)(2,1)S(1)}, bf16[1,1,1,1,64,2048]{5,4,3,2,1,0:T(8,128)(2,1)S(1)}, u32[]{:S(2)}, u32[]{:S(2)}) %collective-permute-start.35) | collective-permute-done | bytes 262176 | tf_op jit(solution)/shard_map/ppermute | solution.py:35
  299.9 7.1 %collective-permute-done.36 = bf16[1,1,1,1,64,2048]{5,4,3,2,1,0:T(8,128)(2,1)S(1)} collective-permute-done((bf16[1,1,1,1,64,2048]{5,4,3,2,1,0:T(8,128)(2,1)S(1)}, bf16[1,1,1,1,64,2048]{5,4,3,2,1,0:T(8,128)(2,1)S(1)}, u32[]{:S(2)}, u32[]{:S(2)}) %collective-permute-start.36) | collective-permute-done | bytes 262176 | tf_op jit(solution)/shard_map/ppermute | solution.py:35
  (204 shorter events, 90.3 us)
Async XLA Ops:
  3.4 22.1 %collective-permute-start.1 = (bf16[1,1,1,1,64,2176]{5,4,3,2,1,0:T(8,128)(2,1)S(1)}, bf16[1,1,1,1,64,2176]{5,4,3,2,1,0:T(8,128)(2,1)S(1)}, u32[]{:S(2)}, u32[]{:S(2)}) collective-permute-start(bf16[1,1,1,1,64,2176]{5,4,3,2,1,0:T(8,128)(2,1)S(1)} %fusion.17), channel_id=1, source_target_pairs={{0,8},{1,9},{2,10},{3,11},{4,12},{5,13},{6,14},{7,15},{8,0},{9,1},... | collective-permute-start | bytes 835592 | tf_op jit(solution)/shard_map/ppermute | solution.py:35
  6.5 24.5 %collective-permute-start.2 = (bf16[1,1,1,1,64,2176]{5,4,3,2,1,0:T(8,128)(2,1)S(1)}, bf16[1,1,1,1,64,2176]{5,4,3,2,1,0:T(8,128)(2,1)S(1)}, u32[]{:S(2)}, u32[]{:S(2)}) collective-permute-start(bf16[1,1,1,1,64,2176]{5,4,3,2,1,0:T(8,128)(2,1)S(1)} %fusion.17), channel_id=1, source_target_pairs={{0,12},{1,13},{2,14},{3,15},{4,8},{5,9},{6,10},{7,11},{8,4},{9,5},... | collective-permute-start | bytes 835592 | tf_op jit(solution)/shard_map/ppermute | solution.py:35
  32.8 21.3 %collective-permute-start.5 = (bf16[1,1,1,1,64,2048]{5,4,3,2,1,0:T(8,128)(2,1)S(1)}, bf16[1,1,1,1,64,2048]{5,4,3,2,1,0:T(8,128)(2,1)}, u32[]{:S(2)}, u32[]{:S(2)}) collective-permute-start(bf16[1,1,1,1,64,2048]{5,4,3,2,1,0:T(8,128)(2,1)S(1)} %dynamic-slice_bitcast_fusion), channel_id=1, source_target_pairs={{0,4},{1,5},{2,6},{3,7},{4,0},{5,1},{6,2},{7,3},{8,12},{9,13},{10,... | collective-permute-start | bytes 786440 | tf_op jit(solution)/shard_map/ppermute | solution.py:35
  32.8 21.3 %collective-permute-start.6 = (bf16[1,1,1,1,64,2048]{5,4,3,2,1,0:T(8,128)(2,1)S(1)}, bf16[1,1,1,1,64,2048]{5,4,3,2,1,0:T(8,128)(2,1)}, u32[]{:S(2)}, u32[]{:S(2)}) collective-permute-start(bf16[1,1,1,1,64,2048]{5,4,3,2,1,0:T(8,128)(2,1)S(1)} %dynamic-slice_bitcast_fusion), channel_id=1, source_target_pairs={{0,8},{1,9},{2,10},{3,11},{4,12},{5,13},{6,14},{7,15},{8,0},{9,1},... | collective-permute-start | bytes 786440 | tf_op jit(solution)/shard_map/ppermute | solution.py:35
  35.9 21.8 %collective-permute-start.7 = (bf16[1,1,1,1,64,2048]{5,4,3,2,1,0:T(8,128)(2,1)S(1)}, bf16[1,1,1,1,64,2048]{5,4,3,2,1,0:T(8,128)(2,1)}, u32[]{:S(2)}, u32[]{:S(2)}) collective-permute-start(bf16[1,1,1,1,64,2048]{5,4,3,2,1,0:T(8,128)(2,1)S(1)} %dynamic-slice_bitcast_fusion), channel_id=1, source_target_pairs={{0,12},{1,13},{2,14},{3,15},{4,8},{5,9},{6,10},{7,11},{8,4},{9,5},... | collective-permute-start | bytes 786440 | tf_op jit(solution)/shard_map/ppermute | solution.py:35
  36.3 16.3 %collective-permute-start.3 = (bf16[1,1,4,1,64,1152]{5,4,3,2,1,0:T(8,128)(2,1)S(1)}, bf16[1,1,4,1,64,1152]{5,4,3,2,1,0:T(8,128)(2,1)S(1)}, u32[]{:S(2)}, u32[]{:S(2)}) collective-permute-start(bf16[1,1,4,1,64,1152]{5,4,3,2,1,0:T(8,128)(2,1)S(1)} %slice.388), channel_id=1, source_target_pairs={{0,16},{16,0},{1,17},{17,1},{2,18},{18,2},{3,19},{19,3},{4,20},{20... | collective-permute-start | bytes 1769480 | tf_op jit(solution)/shard_map/ppermute | solution.py:35
  44.2 27.4 %collective-permute-start.9 = (bf16[1,2,4,1,64,1024]{5,4,3,2,1,0:T(8,128)(2,1)S(1)}, bf16[1,2,4,1,64,1024]{5,4,3,2,1,0:T(8,128)(2,1)S(1)}, u32[]{:S(2)}, u32[]{:S(2)}) collective-permute-start(bf16[1,2,4,1,64,1024]{5,4,3,2,1,0:T(8,128)(2,1)S(1)} %pad_maximum_fusion.7), channel_id=1, source_target_pairs={{0,16},{16,0},{1,17},{17,1},{2,18},{18,2},{3,19},{19,3},{4,20},{20... | collective-permute-start | bytes 3145736 | tf_op jit(solution)/shard_map/ppermute | solution.py:35
  52.7 21.2 %collective-permute-start.4 = (bf16[1,1,4,2,64,1152]{5,4,3,2,1,0:T(8,128)(2,1)S(1)}, bf16[1,1,4,2,64,1152]{5,4,3,2,1,0:T(8,128)(2,1)S(1)}, u32[]{:S(2)}, u32[]{:S(2)}) collective-permute-start(bf16[1,1,4,2,64,1152]{5,4,3,2,1,0:T(8,128)(2,1)S(1)} %pad_maximum_fusion.4), channel_id=1, source_target_pairs={{0,2},{1,3},{2,0},{3,1},{4,6},{5,7},{6,4},{7,5},{8,10},{9,11},{10,... | collective-permute-start | bytes 3538952 | tf_op jit(solution)/shard_map/ppermute | solution.py:35
  73.1 38.4 %collective-permute-start.13 = (bf16[1024,1024]{1,0:T(8,128)(2,1)}, bf16[1024,1024]{1,0:T(8,128)(2,1)}, u32[]{:S(2)}, u32[]{:S(2)}) collective-permute-start(bf16[1024,1024]{1,0:T(8,128)(2,1)} %bitcast.7.xb_ref.xb0), channel_id=1, source_target_pairs={{0,1},{1,0},{2,3},{3,2},{4,5},{5,4},{6,7},{7,6},{8,9},{9,8},{10,11... | collective-permute-start | bytes 6291464 | tf_op jit(solution)/shard_map/ppermute | solution.py:35
  74.9 36.7 %collective-permute-start.12 = (bf16[1024,1152]{1,0:T(8,128)(2,1)S(1)}, bf16[1024,1152]{1,0:T(8,128)(2,1)}, u32[]{:S(2)}, u32[]{:S(2)}) collective-permute-start(bf16[1024,1152]{1,0:T(8,128)(2,1)S(1)} %bitcast.73), channel_id=1, source_target_pairs={{0,1},{1,0},{2,3},{3,2},{4,5},{5,4},{6,7},{7,6},{8,9},{9,8},{10,11... | collective-permute-start | bytes 7077896 | tf_op jit(solution)/shard_map/ppermute | solution.py:35
  74.9 15.2 %collective-permute-start.10 = (bf16[1,1,4,1,64,1024]{5,4,3,2,1,0:T(8,128)(2,1)S(1)}, bf16[1,1,4,1,64,1024]{5,4,3,2,1,0:T(8,128)(2,1)}, u32[]{:S(2)}, u32[]{:S(2)}) collective-permute-start(bf16[1,1,4,1,64,1024]{5,4,3,2,1,0:T(8,128)(2,1)S(1)} %get-tuple-element.111), channel_id=1, source_target_pairs={{0,16},{16,0},{1,17},{17,1},{2,18},{18,2},{3,19},{19,3},{4,20},{20... | collective-permute-start | bytes 1572872 | tf_op jit(solution)/shard_map/ppermute | solution.py:35
  92.4 39.0 %collective-permute-start.17 = (bf16[1,2,4,1,64,1024]{5,4,3,2,1,0:T(8,128)(2,1)}, bf16[1,2,4,1,64,1024]{5,4,3,2,1,0:T(8,128)(2,1)}, u32[]{:S(2)}, u32[]{:S(2)}) collective-permute-start(bf16[1,2,4,1,64,1024]{5,4,3,2,1,0:T(8,128)(2,1)} %pad_maximum_fusion.9), channel_id=1, source_target_pairs={{0,16},{16,0},{1,17},{17,1},{2,18},{18,2},{3,19},{19,3},{4,20},{20... | collective-permute-start | bytes 3145736 | tf_op jit(solution)/shard_map/ppermute | solution.py:35
  93.8 39.1 %collective-permute-start.16 = (bf16[1,1,4,2,64,1024]{5,4,3,2,1,0:T(8,128)(2,1)}, bf16[1,1,4,2,64,1024]{5,4,3,2,1,0:T(8,128)(2,1)}, u32[]{:S(2)}, u32[]{:S(2)}) collective-permute-start(bf16[1,1,4,2,64,1024]{5,4,3,2,1,0:T(8,128)(2,1)} %pad_maximum_fusion.8), channel_id=1, source_target_pairs={{0,2},{1,3},{2,0},{3,1},{4,6},{5,7},{6,4},{7,5},{8,10},{9,11},{10,... | collective-permute-start | bytes 3145736 | tf_op jit(solution)/shard_map/ppermute | solution.py:35
  135.3 28.4 %collective-permute-start.20 = (bf16[1024,1024]{1,0:T(8,128)(2,1)S(1)}, bf16[1024,1024]{1,0:T(8,128)(2,1)S(1)}, u32[]{:S(2)}, u32[]{:S(2)}) collective-permute-start(bf16[1024,1024]{1,0:T(8,128)(2,1)S(1)} %bitcast.76), channel_id=1, source_target_pairs={{0,1},{1,0},{2,3},{3,2},{4,5},{5,4},{6,7},{7,6},{8,9},{9,8},{10,11... | collective-permute-start | bytes 6291464 | tf_op jit(solution)/shard_map/ppermute | solution.py:35
  135.4 28.4 %collective-permute-start.19 = (bf16[1024,1024]{1,0:T(8,128)(2,1)S(1)}, bf16[1024,1024]{1,0:T(8,128)(2,1)}, u32[]{:S(2)}, u32[]{:S(2)}) collective-permute-start(bf16[1024,1024]{1,0:T(8,128)(2,1)S(1)} %bitcast.79), channel_id=1, source_target_pairs={{0,1},{1,0},{2,3},{3,2},{4,5},{5,4},{6,7},{7,6},{8,9},{9,8},{10,11... | collective-permute-start | bytes 6291464 | tf_op jit(solution)/shard_map/ppermute | solution.py:35
  135.9 20.3 %collective-permute-start.14 = (bf16[1,2,4,2,64,1024]{5,4,3,2,1,0:T(8,128)(2,1)}, bf16[1,2,4,2,64,1024]{5,4,3,2,1,0:T(8,128)(2,1)}, u32[]{:S(2)}, u32[]{:S(2)}) collective-permute-start(bf16[1,2,4,2,64,1024]{5,4,3,2,1,0:T(8,128)(2,1)} %bitcast.18), channel_id=1, source_target_pairs={{0,1},{1,0},{2,3},{3,2},{4,5},{5,4},{6,7},{7,6},{8,9},{9,8},{10,11... | collective-permute-start | bytes 6291464 | tf_op jit(solution)/shard_map/ppermute | solution.py:35
  135.9 20.2 %collective-permute-start.15 = (bf16[1,2,4,2,64,1024]{5,4,3,2,1,0:T(8,128)(2,1)}, bf16[1,2,4,2,64,1024]{5,4,3,2,1,0:T(8,128)(2,1)}, u32[]{:S(2)}, u32[]{:S(2)}) collective-permute-start(bf16[1,2,4,2,64,1024]{5,4,3,2,1,0:T(8,128)(2,1)} %bitcast.19), channel_id=1, source_target_pairs={{0,1},{1,0},{2,3},{3,2},{4,5},{5,4},{6,7},{7,6},{8,9},{9,8},{10,11... | collective-permute-start | bytes 6291464 | tf_op jit(solution)/shard_map/ppermute | solution.py:35
  159.2 25.4 %collective-permute-start.21 = (bf16[1,2,4,1,64,1024]{5,4,3,2,1,0:T(8,128)(2,1)}, bf16[1,2,4,1,64,1024]{5,4,3,2,1,0:T(8,128)(2,1)}, u32[]{:S(2)}, u32[]{:S(2)}) collective-permute-start(bf16[1,2,4,1,64,1024]{5,4,3,2,1,0:T(8,128)(2,1)} %add_convert_fusion.2), channel_id=1, source_target_pairs={{0,16},{16,0},{1,17},{17,1},{2,18},{18,2},{3,19},{19,3},{4,20},{20... | collective-permute-start | bytes 3145736 | tf_op jit(solution)/shard_map/ppermute | solution.py:35
  162.4 24.9 %collective-permute-start.18 = (bf16[1,1,4,2,64,1024]{5,4,3,2,1,0:T(8,128)(2,1)}, bf16[1,1,4,2,64,1024]{5,4,3,2,1,0:T(8,128)(2,1)}, u32[]{:S(2)}, u32[]{:S(2)}) collective-permute-start(bf16[1,1,4,2,64,1024]{5,4,3,2,1,0:T(8,128)(2,1)} %add_convert_fusion.3), channel_id=1, source_target_pairs={{0,2},{1,3},{2,0},{3,1},{4,6},{5,7},{6,4},{7,5},{8,10},{9,11},{10,... | collective-permute-start | bytes 3145736 | tf_op jit(solution)/shard_map/ppermute | solution.py:35
  189.7 22.8 %collective-permute-start.23 = (bf16[1,2,4,2,64,1024]{5,4,3,2,1,0:T(8,128)(2,1)}, bf16[1,2,4,2,64,1024]{5,4,3,2,1,0:T(8,128)(2,1)}, u32[]{:S(2)}, u32[]{:S(2)}) collective-permute-start(bf16[1,2,4,2,64,1024]{5,4,3,2,1,0:T(8,128)(2,1)} %bitcast.23), channel_id=1, source_target_pairs={{0,1},{1,0},{2,3},{3,2},{4,5},{5,4},{6,7},{7,6},{8,9},{9,8},{10,11... | collective-permute-start | bytes 6291464 | tf_op jit(solution)/shard_map/ppermute | solution.py:35
  189.7 22.9 %collective-permute-start.24 = (bf16[1,2,4,2,64,1024]{5,4,3,2,1,0:T(8,128)(2,1)}, bf16[1,2,4,2,64,1024]{5,4,3,2,1,0:T(8,128)(2,1)}, u32[]{:S(2)}, u32[]{:S(2)}) collective-permute-start(bf16[1,2,4,2,64,1024]{5,4,3,2,1,0:T(8,128)(2,1)} %bitcast.24), channel_id=1, source_target_pairs={{0,1},{1,0},{2,3},{3,2},{4,5},{5,4},{6,7},{7,6},{8,9},{9,8},{10,11... | collective-permute-start | bytes 6291464 | tf_op jit(solution)/shard_map/ppermute | solution.py:35
  197.9 19.5 %collective-permute-start.25 = (bf16[1,1,4,1,64,1024]{5,4,3,2,1,0:T(8,128)(2,1)}, bf16[1,1,4,1,64,1024]{5,4,3,2,1,0:T(8,128)(2,1)S(1)}, u32[]{:S(2)}, u32[]{:S(2)}) collective-permute-start(bf16[1,1,4,1,64,1024]{5,4,3,2,1,0:T(8,128)(2,1)} %add_convert_fusion.6), channel_id=1, source_target_pairs={{0,2},{1,3},{2,0},{3,1},{4,6},{5,7},{6,4},{7,5},{8,10},{9,11},{10,... | collective-permute-start | bytes 1572872 | tf_op jit(solution)/shard_map/ppermute | solution.py:35
  199.2 18.1 %collective-permute-start.22 = (bf16[1,1,4,1,64,1024]{5,4,3,2,1,0:T(8,128)(2,1)}, bf16[1,1,4,1,64,1024]{5,4,3,2,1,0:T(8,128)(2,1)}, u32[]{:S(2)}, u32[]{:S(2)}) collective-permute-start(bf16[1,1,4,1,64,1024]{5,4,3,2,1,0:T(8,128)(2,1)} %add_convert_fusion.7), channel_id=1, source_target_pairs={{0,16},{16,0},{1,17},{17,1},{2,18},{18,2},{3,19},{19,3},{4,20},{20... | collective-permute-start | bytes 1572872 | tf_op jit(solution)/shard_map/ppermute | solution.py:35
  220.5 24.8 %collective-permute-start.30 = (bf16[1,2,4,1,64,1024]{5,4,3,2,1,0:T(8,128)(2,1)}, bf16[1,2,4,1,64,1024]{5,4,3,2,1,0:T(8,128)(2,1)}, u32[]{:S(2)}, u32[]{:S(2)}) collective-permute-start(bf16[1,2,4,1,64,1024]{5,4,3,2,1,0:T(8,128)(2,1)} %add_convert_fusion), channel_id=1, source_target_pairs={{0,16},{16,0},{1,17},{17,1},{2,18},{18,2},{3,19},{19,3},{4,20},{20... | collective-permute-start | bytes 3145736 | tf_op jit(solution)/shard_map/ppermute | solution.py:35
  221.0 26.7 %collective-permute-start.29 = (bf16[1,1,4,2,64,1024]{5,4,3,2,1,0:T(8,128)(2,1)S(1)}, bf16[1,1,4,2,64,1024]{5,4,3,2,1,0:T(8,128)(2,1)}, u32[]{:S(2)}, u32[]{:S(2)}) collective-permute-start(bf16[1,1,4,2,64,1024]{5,4,3,2,1,0:T(8,128)(2,1)S(1)} %add_convert_fusion.1), channel_id=1, source_target_pairs={{0,2},{1,3},{2,0},{3,1},{4,6},{5,7},{6,4},{7,5},{8,10},{9,11},{10,... | collective-permute-start | bytes 3145736 | tf_op jit(solution)/shard_map/ppermute | solution.py:35
  221.7 40.0 %collective-permute-start.27 = (bf16[1,1,1,1,64,2048]{5,4,3,2,1,0:T(8,128)(2,1)}, bf16[1,1,1,1,64,2048]{5,4,3,2,1,0:T(8,128)(2,1)}, u32[]{:S(2)}, u32[]{:S(2)}) collective-permute-start(bf16[1,1,1,1,64,2048]{5,4,3,2,1,0:T(8,128)(2,1)} %get-tuple-element.233), channel_id=1, source_target_pairs={{0,8},{1,9},{2,10},{3,11},{4,12},{5,13},{6,14},{7,15},{8,0},{9,1},... | collective-permute-start | bytes 786440 | tf_op jit(solution)/shard_map/ppermute | solution.py:35
  224.2 37.5 %collective-permute-start.28 = (bf16[1,1,1,1,64,2048]{5,4,3,2,1,0:T(8,128)(2,1)}, bf16[1,1,1,1,64,2048]{5,4,3,2,1,0:T(8,128)(2,1)}, u32[]{:S(2)}, u32[]{:S(2)}) collective-permute-start(bf16[1,1,1,1,64,2048]{5,4,3,2,1,0:T(8,128)(2,1)} %get-tuple-element.232), channel_id=1, source_target_pairs={{0,12},{1,13},{2,14},{3,15},{4,8},{5,9},{6,10},{7,11},{8,4},{9,5},... | collective-permute-start | bytes 786440 | tf_op jit(solution)/shard_map/ppermute | solution.py:35
  224.8 37.0 %collective-permute-start.26 = (bf16[1,1,1,1,64,2048]{5,4,3,2,1,0:T(8,128)(2,1)}, bf16[1,1,1,1,64,2048]{5,4,3,2,1,0:T(8,128)(2,1)}, u32[]{:S(2)}, u32[]{:S(2)}) collective-permute-start(bf16[1,1,1,1,64,2048]{5,4,3,2,1,0:T(8,128)(2,1)} %add_convert_fusion.15), channel_id=1, source_target_pairs={{0,4},{1,5},{2,6},{3,7},{4,0},{5,1},{6,2},{7,3},{8,12},{9,13},{10,... | collective-permute-start | bytes 786440 | tf_op jit(solution)/shard_map/ppermute | solution.py:35
  252.1 56.7 %all-to-all-start = ((bf16[16,266,128]{2,1,0:T(8,128)(2,1)}), bf16[16,266,128]{2,1,0:T(8,128)(2,1)}, u32[]{:S(2)}, u32[]{:S(2)}) async-start(bf16[16,266,128]{2,1,0:T(8,128)(2,1)} %maximum_bitcast_fusion), calls=%async_computation | async-start | bytes 2228224 | tf_op jit(solution)/shard_map/all_to_all | solution.py:467
  265.9 34.0 %collective-permute-start.35 = (bf16[1,1,1,1,64,2048]{5,4,3,2,1,0:T(8,128)(2,1)S(1)}, bf16[1,1,1,1,64,2048]{5,4,3,2,1,0:T(8,128)(2,1)S(1)}, u32[]{:S(2)}, u32[]{:S(2)}) collective-permute-start(bf16[1,1,1,1,64,2048]{5,4,3,2,1,0:T(8,128)(2,1)S(1)} %add_convert_fusion.10), channel_id=1, source_target_pairs={{0,8},{1,9},{2,10},{3,11},{4,12},{5,13},{6,14},{7,15},{8,0},{9,1},... | collective-permute-start | bytes 786440 | tf_op jit(solution)/shard_map/ppermute | solution.py:35
  270.4 29.5 %collective-permute-start.34 = (bf16[1,1,1,1,64,2048]{5,4,3,2,1,0:T(8,128)(2,1)S(1)}, bf16[1,1,1,1,64,2048]{5,4,3,2,1,0:T(8,128)(2,1)S(1)}, u32[]{:S(2)}, u32[]{:S(2)}) collective-permute-start(bf16[1,1,1,1,64,2048]{5,4,3,2,1,0:T(8,128)(2,1)S(1)} %get-tuple-element.231), channel_id=1, source_target_pairs={{0,4},{1,5},{2,6},{3,7},{4,0},{5,1},{6,2},{7,3},{8,12},{9,13},{10,... | collective-permute-start | bytes 786440 | tf_op jit(solution)/shard_map/ppermute | solution.py:35
  270.4 36.6 %collective-permute-start.36 = (bf16[1,1,1,1,64,2048]{5,4,3,2,1,0:T(8,128)(2,1)S(1)}, bf16[1,1,1,1,64,2048]{5,4,3,2,1,0:T(8,128)(2,1)S(1)}, u32[]{:S(2)}, u32[]{:S(2)}) collective-permute-start(bf16[1,1,1,1,64,2048]{5,4,3,2,1,0:T(8,128)(2,1)S(1)} %get-tuple-element.230), channel_id=1, source_target_pairs={{0,12},{1,13},{2,14},{3,15},{4,8},{5,9},{6,10},{7,11},{8,4},{9,5},... | collective-permute-start | bytes 786440 | tf_op jit(solution)/shard_map/ppermute | solution.py:35
  (30 other events, 321.7 us)
